TPU v7x, 32 devices: a whole 2x2x4 slice. The times are simulated.
32 devices in a mesh: grp: 4 (over z), shard: 8 (over y, x, core).
Axes of the slice: x: 2, y: 2, z: 4, core: 2. Of those that a mesh axis runs over, the one named last changes fastest.
Arguments:
- inputs: bfloat16 [128, 192, 1024], P(('grp', 'shard')), may hold values from -6 to 6
- cotangent: bfloat16 [128, 192, 1024], P(('grp', 'shard')), may hold values from -6 to 6
- lengths: int32 [128], replicated, may hold values from 1 to 192, as said below
- dealing: int32 [128], replicated, may hold values from 0 to 127, as said below
- g_attn: bfloat16 [1024], P(('grp', 'shard')), may hold values from 0.099609375 to 1.8984375
- w_query: bfloat16 [1024, 512], P(('grp', 'shard')), may hold values from -0.1875 to 0.1875
- w_key: bfloat16 [1024, 512], P(('grp', 'shard')), may hold values from -0.1875 to 0.1875
- w_value: bfloat16 [1024, 1024], P(('grp', 'shard')), may hold values from -0.1875 to 0.1875
- w_outgate: bfloat16 [1024, 1024], P(('grp', 'shard')), may hold values from -0.1875 to 0.1875
- w_lowrank: bfloat16 [1024, 16], P(('grp', 'shard')), may hold values from -0.1875 to 0.1875
- w_forget: bfloat16 [16, 512], P(None, ('grp', 'shard')), may hold values from -0.75 to 0.75
- b_forget: bfloat16 [512], P(('grp', 'shard')), may hold values from -1 to 5
- g_head: bfloat16 [256], P(('grp', 'shard')), may hold values from 0.099609375 to 1.8984375
- w_output: bfloat16 [1024, 1024], P(('grp', 'shard')), may hold values from -0.25 to 0.25
- g_ffn: bfloat16 [1024], P(('grp', 'shard')), may hold values from 0.099609375 to 1.8984375
- w_gate: bfloat16 [1024, 2816], P(('grp', 'shard')), may hold values from -0.1875 to 0.1875
- w_up: bfloat16 [1024, 2816], P(('grp', 'shard')), may hold values from -0.1875 to 0.1875
- w_down: bfloat16 [2816, 1024], P(None, ('grp', 'shard')), may hold values from -0.15625 to 0.15625
Outputs:
- output: bfloat16 [128, 192, 1024], P(('grp', 'shard'))
- grad_input: bfloat16 [128, 192, 1024], P(('grp', 'shard'))
- dg_attn: float32 [1024], P(('grp', 'shard'))
- dw_query: float32 [1024, 512], P(('grp', 'shard'))
- dw_key: float32 [1024, 512], P(('grp', 'shard'))
- dw_value: float32 [1024, 1024], P(('grp', 'shard'))
- dw_outgate: float32 [1024, 1024], P(('grp', 'shard'))
- dw_lowrank: float32 [1024, 16], P(('grp', 'shard'))
- dw_forget: float32 [16, 512], P(None, ('grp', 'shard'))
- db_forget: float32 [512], P(('grp', 'shard'))
- dg_head: float32 [256], P(('grp', 'shard'))
- dw_output: float32 [1024, 1024], P(('grp', 'shard'))
- dg_ffn: float32 [1024], P(('grp', 'shard'))
- dw_gate: float32 [1024, 2816], P(('grp', 'shard'))
- dw_up: float32 [1024, 2816], P(('grp', 'shard'))
- dw_down: float32 [2816, 1024], P(None, ('grp', 'shard'))
Inputs may be any that keep to these rules, and one draw needn't show every extreme that they name: dealing[q], for slot q = (m * 32 + r) * 2 + k, is the given position of the sequence that device r takes as its k-th in micro-batch m; a device's given positions are its 4 rows of inputs, and that sequence lies on a device with r's index along shard, at one of its given positions m * 2 to (m + 1) * 2 - 1. Each position is dealt once, and no device deals two sequences of one micro-batch to the same device. lengths[q] is the length of the sequence of slot q (slots as for dealing). Of the 2 slots of one device and micro-batch, exactly one holds 129 to 192 tokens, which take 3 blocks of 64 positions, and each other slot holds 1 to 64 tokens, one block; so the blocks of one device and micro-batch number 4 exactly. Some sequence has exactly 192 tokens.
All inputs are finite; a program needn't handle non-finite values.
Results may differ from a plain program's by a relative error of at most 0.02.
Values may be sent and summed in bfloat16 or wider, within the bound.
A program may use at most 192 MiB of HBM per device.

v0:
```python
import jax
import jax.numpy as jnp
from jax import lax
from jax.sharding import PartitionSpec as P

D = 1024
HEADS = 4
BLOCK = 64
BIN_BLOCKS = 4
SEQ_BIN = 2
MB = 2


EPS = 1e-05
HEAD_EPS = 1.0


def matmul(left_mat, right_mat):
    return jnp.dot(left_mat, right_mat, preferred_element_type=jnp.float32)


def rows_contract(left_mat, right_mat):
    return lax.dot_general(
        left_mat, right_mat, (((0,), (0,)), ((), ())), preferred_element_type=jnp.float32
    )


def right_transpose(left_mat, right_mat):
    return lax.dot_general(
        left_mat, right_mat, (((1,), (1,)), ((), ())), preferred_element_type=jnp.float32
    )


def scaled_rows(rows_in, gain_vec):
    return rows_in * lax.rsqrt(jnp.mean(rows_in * rows_in, axis=-1, keepdims=True) + EPS) * gain_vec


def head_rows(rows_in, gain_vec):
    return (
        rows_in
        * lax.rsqrt(jnp.mean(rows_in * rows_in, axis=-1, keepdims=True) + HEAD_EPS)
        * gain_vec
    )


def forget_rate(logits):
    return jax.nn.log_sigmoid(logits) / 16.0


def swiglu_core(pre_gate, pre_up):
    return jax.nn.silu(pre_gate) * pre_up


def head_gate(mixed_out, gate_out, head_gain):
    normed = head_rows(mixed_out, head_gain)
    active = gate_out * jax.nn.sigmoid(gate_out)
    return normed.reshape(active.shape) * active


def block_gates(queries, key_rows, forget):
    running = jnp.cumsum(forget, axis=1)
    tail_sum = running[:, -1:]
    q_gate = queries * queries.shape[-1] ** (-0.5) * jnp.exp(running)
    k_back = key_rows * jnp.exp(-running)
    k_tail = key_rows * jnp.exp(tail_sum - running)
    return (q_gate, k_back, k_tail, jnp.exp(tail_sum[:, 0]))


def split_axis(array_in, axis_pos, parts):
    shape_in = array_in.shape
    return array_in.reshape(
        shape_in[:axis_pos] + (parts, shape_in[axis_pos] // parts) + shape_in[axis_pos + 1 :]
    )


def join_axis(array_in, axis_pos):
    shape_in = array_in.shape
    return array_in.reshape(
        shape_in[:axis_pos]
        + (shape_in[axis_pos] * shape_in[axis_pos + 1],)
        + shape_in[axis_pos + 2 :]
    )


def layer_pass(weights, rows_in, back_in, block_starts):
    (
        g_attn,
        w_query,
        w_key,
        w_value,
        w_outgate,
        w_lowrank,
        w_forget,
        b_forget,
        g_head,
        w_output,
        g_ffn,
        w_gate,
        w_up,
        w_down,
    ) = weights
    row_count = rows_in.shape[0]
    blocks = row_count // BLOCK
    key_dim = w_query.shape[1] // HEADS
    val_dim = w_value.shape[1] // HEADS
    key_shape = (blocks, BLOCK, HEADS, key_dim)
    val_shape = (blocks, BLOCK, HEADS, val_dim)
    flat_rows = rows_in.astype(jnp.float32)
    norm_one, pull_one = jax.vjp(scaled_rows, flat_rows, g_attn.astype(jnp.float32))
    xn_one = norm_one.astype(jnp.bfloat16)
    queries = matmul(xn_one, w_query)
    key_rows = matmul(xn_one, w_key)
    values = matmul(xn_one, w_value).astype(jnp.bfloat16)
    gate_out = matmul(xn_one, w_outgate)
    lowrank = matmul(xn_one, w_lowrank).astype(jnp.bfloat16)
    logits = matmul(lowrank, w_forget) + b_forget.astype(jnp.float32)
    forget, pull_forget = jax.vjp(forget_rate, logits)
    gate_vals, pull_gates = jax.vjp(
        block_gates,
        queries.reshape(key_shape),
        key_rows.reshape(key_shape),
        forget.reshape(key_shape),
    )
    q_gate = gate_vals[0].astype(jnp.bfloat16)
    k_back = gate_vals[1].astype(jnp.bfloat16)
    k_tail = gate_vals[2].astype(jnp.bfloat16)
    decays = gate_vals[3]
    val_blocks = values.reshape(val_shape)
    spot_ids = jnp.arange(BLOCK)
    causal = (spot_ids[:, None] >= spot_ids[None, :]).astype(jnp.float32)
    scores = jnp.einsum("cthd,cshd->chts", q_gate, k_back, preferred_element_type=jnp.float32)
    attn_probs = (scores * causal).astype(jnp.bfloat16)
    intra_out = jnp.einsum(
        "chts,cshe->cthe", attn_probs, val_blocks, preferred_element_type=jnp.float32
    )
    update = jnp.einsum("cthd,cthe->chde", k_tail, val_blocks, preferred_element_type=jnp.float32)

    def advance(carried, block_item):
        factor, upd_block, is_start = block_item
        carried = jnp.where(is_start, 0.0, carried)
        return (factor[..., None] * carried + upd_block, carried)

    zero_state = jnp.zeros((HEADS, key_dim, val_dim), jnp.float32)
    _, before = lax.scan(advance, zero_state, (decays, update, block_starts))
    before_low = before.astype(jnp.bfloat16)
    inter_out = jnp.einsum(
        "cthd,chde->cthe", q_gate, before_low, preferred_element_type=jnp.float32
    )
    mixed_out = (intra_out + inter_out).reshape(row_count, HEADS, val_dim)
    gated_f, pull_head = jax.vjp(head_gate, mixed_out, gate_out, g_head.astype(jnp.float32))
    gated_out = gated_f.astype(jnp.bfloat16)
    resid_one = flat_rows + matmul(gated_out, w_output)
    norm_two, pull_two = jax.vjp(scaled_rows, resid_one, g_ffn.astype(jnp.float32))
    xn_two = norm_two.astype(jnp.bfloat16)
    pre_gate = matmul(xn_two, w_gate)
    pre_up = matmul(xn_two, w_up)
    hidden_f, pull_ffn = jax.vjp(swiglu_core, pre_gate, pre_up)
    hidden = hidden_f.astype(jnp.bfloat16)
    output = (resid_one + matmul(hidden, w_down)).astype(jnp.bfloat16)
    back_f = back_in.astype(jnp.float32)
    dw_down = rows_contract(hidden, back_in)
    d_hidden = right_transpose(back_in, w_down)
    d_pre_gate, d_pre_up = pull_ffn(d_hidden)
    d_gate_low = d_pre_gate.astype(jnp.bfloat16)
    d_up_low = d_pre_up.astype(jnp.bfloat16)
    dw_gate = rows_contract(xn_two, d_gate_low)
    dw_up = rows_contract(xn_two, d_up_low)
    d_norm_two = right_transpose(d_gate_low, w_gate) + right_transpose(d_up_low, w_up)
    d_resid_part, dg_ffn = pull_two(d_norm_two)
    d_resid = back_f + d_resid_part
    d_attn = d_resid.astype(jnp.bfloat16)
    dw_output = rows_contract(gated_out, d_attn)
    d_gated = right_transpose(d_attn, w_output)
    d_mixed_f, d_gate_out_f, dg_head = pull_head(d_gated)
    d_mixed = d_mixed_f.astype(jnp.bfloat16).reshape(val_shape)
    d_scores = jnp.einsum(
        "cthe,cshe->chts", d_mixed, val_blocks, preferred_element_type=jnp.float32
    )
    d_probs = (d_scores * causal).astype(jnp.bfloat16)
    d_q_gate = jnp.einsum(
        "chts,cshd->cthd", d_probs, k_back, preferred_element_type=jnp.float32
    ) + jnp.einsum("cthe,chde->cthd", d_mixed, before_low, preferred_element_type=jnp.float32)
    d_k_back = jnp.einsum("chts,cthd->cshd", d_probs, q_gate, preferred_element_type=jnp.float32)
    d_val_intra = jnp.einsum(
        "chts,cthe->cshe", attn_probs, d_mixed, preferred_element_type=jnp.float32
    )
    d_before = jnp.einsum("cthd,cthe->chde", q_gate, d_mixed, preferred_element_type=jnp.float32)

    def retreat(d_after, block_item):
        factor, carried, d_state, is_start = block_item
        d_decay = jnp.sum(d_after * carried, axis=-1)
        flowing = d_state + factor[..., None] * d_after
        return (jnp.where(is_start, 0.0, flowing), (d_after, d_decay))

    _, (d_update, d_decays) = lax.scan(
        retreat, zero_state, (decays, before, d_before, block_starts), reverse=True
    )
    d_update_low = d_update.astype(jnp.bfloat16)
    d_k_tail = jnp.einsum(
        "cthe,chde->cthd", val_blocks, d_update_low, preferred_element_type=jnp.float32
    )
    d_values = (
        (
            d_val_intra
            + jnp.einsum(
                "cthd,chde->cthe", k_tail, d_update_low, preferred_element_type=jnp.float32
            )
        )
        .reshape(row_count, -1)
        .astype(jnp.bfloat16)
    )
    d_query_f, d_key_f, d_forget = pull_gates((d_q_gate, d_k_back, d_k_tail, d_decays))
    d_queries = d_query_f.reshape(row_count, -1).astype(jnp.bfloat16)
    d_keys = d_key_f.reshape(row_count, -1).astype(jnp.bfloat16)
    (d_logits,) = pull_forget(d_forget.reshape(row_count, -1))
    db_forget = jnp.sum(d_logits, axis=0)
    d_logit_low = d_logits.astype(jnp.bfloat16)
    dw_forget = rows_contract(lowrank, d_logit_low)
    d_lowrank = right_transpose(d_logit_low, w_forget).astype(jnp.bfloat16)
    d_gate_out = d_gate_out_f.astype(jnp.bfloat16)
    dw_query = rows_contract(xn_one, d_queries)
    dw_key = rows_contract(xn_one, d_keys)
    dw_value = rows_contract(xn_one, d_values)
    dw_outgate = rows_contract(xn_one, d_gate_out)
    dw_lowrank = rows_contract(xn_one, d_lowrank)
    d_norm_one = (
        right_transpose(d_queries, w_query)
        + right_transpose(d_keys, w_key)
        + right_transpose(d_values, w_value)
        + right_transpose(d_gate_out, w_outgate)
        + right_transpose(d_lowrank, w_lowrank)
    )
    d_flat, dg_attn = pull_one(d_norm_one)
    grad_rows = (d_resid + d_flat).astype(jnp.bfloat16)
    grads = (
        dg_attn,
        dw_query,
        dw_key,
        dw_value,
        dw_outgate,
        dw_lowrank,
        dw_forget,
        db_forget,
        dg_head,
        dw_output,
        dg_ffn,
        dw_gate,
        dw_up,
        dw_down,
    )
    return (output, grad_rows, grads)


def shards(
    inputs,
    cotangent,
    lengths,
    dealing,
    g_attn,
    w_query,
    w_key,
    w_value,
    w_outgate,
    w_lowrank,
    w_forget,
    b_forget,
    g_head,
    w_output,
    g_ffn,
    w_gate,
    w_up,
    w_down,
):
    grp_count = lax.axis_size("grp")
    shard_count = lax.axis_size("shard")
    devices = grp_count * shard_count
    self_index = lax.axis_index("grp") * shard_count + lax.axis_index("shard")
    seq_dev = inputs.shape[0]
    max_len = inputs.shape[1]
    seq_total = dealing.shape[0]
    bin_rows = BIN_BLOCKS * BLOCK
    places = jnp.arange(SEQ_BIN, dtype=jnp.int32)
    peer_ids = jnp.arange(grp_count, dtype=jnp.int32)
    spot_ids = jnp.arange(max_len, dtype=jnp.int32)
    row_ids = jnp.arange(bin_rows, dtype=jnp.int32)
    block_ids = row_ids // BLOCK
    block_list = jnp.arange(BIN_BLOCKS, dtype=jnp.int32)
    inverse = (
        jnp.zeros((seq_total,), jnp.int32).at[dealing].set(jnp.arange(seq_total, dtype=jnp.int32))
    )
    zero_low = jnp.zeros((), jnp.bfloat16)
    totals = None
    pieces_out = []
    pieces_grad = []
    for micro_idx in range(MB):
        gathered = (
            lax.all_gather(g_attn, ("grp", "shard"), axis=0, tiled=True),
            lax.all_gather(w_query, ("grp", "shard"), axis=0, tiled=True),
            lax.all_gather(w_key, ("grp", "shard"), axis=0, tiled=True),
            lax.all_gather(w_value, ("grp", "shard"), axis=0, tiled=True),
            lax.all_gather(w_outgate, ("grp", "shard"), axis=0, tiled=True),
            lax.all_gather(w_lowrank, ("grp", "shard"), axis=0, tiled=True),
            lax.all_gather(w_forget, ("grp", "shard"), axis=1, tiled=True),
            lax.all_gather(b_forget, ("grp", "shard"), axis=0, tiled=True),
            lax.all_gather(g_head, ("grp", "shard"), axis=0, tiled=True),
            lax.all_gather(w_output, ("grp", "shard"), axis=0, tiled=True),
            lax.all_gather(g_ffn, ("grp", "shard"), axis=0, tiled=True),
            lax.all_gather(w_gate, ("grp", "shard"), axis=0, tiled=True),
            lax.all_gather(w_up, ("grp", "shard"), axis=0, tiled=True),
            lax.all_gather(w_down, ("grp", "shard"), axis=1, tiled=True),
        )
        first_slot = (micro_idx * devices + self_index) * SEQ_BIN
        taken_ids = lax.dynamic_slice_in_dim(dealing, first_slot, SEQ_BIN)
        seq_len = lax.dynamic_slice_in_dim(lengths, first_slot, SEQ_BIN)
        source_grp = taken_ids // seq_dev // shard_count
        counts = (seq_len + BLOCK - 1) // BLOCK
        offsets = jnp.cumsum(counts) - counts
        inside = (block_ids[:, None] >= offsets[None, :]) & (
            block_ids[:, None] < (offsets + counts)[None, :]
        )
        row_start = jnp.sum(jnp.where(inside, offsets[None, :] * BLOCK, 0), axis=1)
        row_len = jnp.sum(jnp.where(inside, seq_len[None, :], 0), axis=1)
        row_source = jnp.sum(jnp.where(inside, source_grp[None, :], 0), axis=1)
        position = row_ids - row_start
        row_live = position < row_len
        fetch_ids = row_source * max_len + jnp.minimum(position, max_len - 1)
        block_starts = jnp.any(offsets[None, :] == block_list[:, None], axis=1)
        own_given = self_index * seq_dev + micro_idx * SEQ_BIN + places
        target = jnp.take(inverse, own_given)
        target_grp = target // SEQ_BIN % devices // shard_count
        match_out = target_grp[None, :] == peer_ids[:, None]
        has_out = jnp.any(match_out, axis=1)
        chosen = jnp.sum(jnp.where(match_out, places[None, :], 0), axis=1)
        first_seq = micro_idx * SEQ_BIN
        send_rows = jnp.where(
            has_out[:, None, None],
            jnp.take(inputs[first_seq : first_seq + SEQ_BIN], chosen, axis=0),
            zero_low,
        )
        send_back = jnp.where(
            has_out[:, None, None],
            jnp.take(cotangent[first_seq : first_seq + SEQ_BIN], chosen, axis=0),
            zero_low,
        )
        recv_rows, recv_back = (
            lax.all_to_all(send_rows, "grp", split_axis=0, concat_axis=0, tiled=True),
            lax.all_to_all(send_back, "grp", split_axis=0, concat_axis=0, tiled=True),
        )
        packed_rows = jnp.where(
            row_live[:, None], jnp.take(recv_rows.reshape(-1, D), fetch_ids, axis=0), zero_low
        )
        packed_back = jnp.where(
            row_live[:, None], jnp.take(recv_back.reshape(-1, D), fetch_ids, axis=0), zero_low
        )
        out_rows, grad_rows, grads = layer_pass(gathered, packed_rows, packed_back, block_starts)
        if totals is None:
            totals = grads
        else:
            totals = tuple((acc_part + new_part for acc_part, new_part in zip(totals, grads)))
        match_back = source_grp[None, :] == peer_ids[:, None]
        back_start = jnp.sum(jnp.where(match_back, offsets[None, :] * BLOCK, 0), axis=1)
        back_len = jnp.sum(jnp.where(match_back, seq_len[None, :], 0), axis=1)
        keep_back = spot_ids[None, :] < back_len[:, None]
        pull_rows = jnp.minimum(back_start[:, None] + spot_ids[None, :], bin_rows - 1)
        ret_out = jnp.where(keep_back[..., None], jnp.take(out_rows, pull_rows, axis=0), zero_low)
        ret_grad = jnp.where(keep_back[..., None], jnp.take(grad_rows, pull_rows, axis=0), zero_low)
        home_out, home_grad = (
            lax.all_to_all(ret_out, "grp", split_axis=0, concat_axis=0, tiled=True),
            lax.all_to_all(ret_grad, "grp", split_axis=0, concat_axis=0, tiled=True),
        )
        pieces_out.append(jnp.take(home_out, target_grp, axis=0))
        pieces_grad.append(jnp.take(home_grad, target_grp, axis=0))
    out_all = jnp.concatenate(pieces_out, axis=0)
    grad_all = jnp.concatenate(pieces_grad, axis=0)
    grad_dims = (0, 0, 0, 0, 0, 0, 1, 0, 0, 0, 0, 0, 0, 1)
    split_grads = [split_axis(totals[pos], grad_dims[pos], grp_count) for pos in range(14)]
    section_one = (
        lax.psum_scatter(
            split_grads[0].astype(jnp.bfloat16), "shard", scatter_dimension=1, tiled=True
        ).astype(jnp.float32),
        lax.psum_scatter(
            split_grads[1].astype(jnp.bfloat16), "shard", scatter_dimension=1, tiled=True
        ).astype(jnp.float32),
        lax.psum_scatter(
            split_grads[2].astype(jnp.bfloat16), "shard", scatter_dimension=1, tiled=True
        ).astype(jnp.float32),
        lax.psum_scatter(
            split_grads[3].astype(jnp.bfloat16), "shard", scatter_dimension=1, tiled=True
        ).astype(jnp.float32),
        lax.psum_scatter(
            split_grads[4].astype(jnp.bfloat16), "shard", scatter_dimension=1, tiled=True
        ).astype(jnp.float32),
        lax.psum_scatter(
            split_grads[5].astype(jnp.bfloat16), "shard", scatter_dimension=1, tiled=True
        ).astype(jnp.float32),
        lax.psum_scatter(
            split_grads[6].astype(jnp.bfloat16), "shard", scatter_dimension=2, tiled=True
        ).astype(jnp.float32),
        lax.psum_scatter(
            split_grads[7].astype(jnp.bfloat16), "shard", scatter_dimension=1, tiled=True
        ).astype(jnp.float32),
        lax.psum_scatter(
            split_grads[8].astype(jnp.bfloat16), "shard", scatter_dimension=1, tiled=True
        ).astype(jnp.float32),
        lax.psum_scatter(
            split_grads[9].astype(jnp.bfloat16), "shard", scatter_dimension=1, tiled=True
        ).astype(jnp.float32),
        lax.psum_scatter(
            split_grads[10].astype(jnp.bfloat16), "shard", scatter_dimension=1, tiled=True
        ).astype(jnp.float32),
        lax.psum_scatter(
            split_grads[11].astype(jnp.bfloat16), "shard", scatter_dimension=1, tiled=True
        ).astype(jnp.float32),
        lax.psum_scatter(
            split_grads[12].astype(jnp.bfloat16), "shard", scatter_dimension=1, tiled=True
        ).astype(jnp.float32),
        lax.psum_scatter(
            split_grads[13].astype(jnp.bfloat16), "shard", scatter_dimension=2, tiled=True
        ).astype(jnp.float32),
    )
    section_two = (
        lax.psum_scatter(
            section_one[0].astype(jnp.bfloat16), "grp", scatter_dimension=0, tiled=True
        ).astype(jnp.float32),
        lax.psum_scatter(
            section_one[1].astype(jnp.bfloat16), "grp", scatter_dimension=0, tiled=True
        ).astype(jnp.float32),
        lax.psum_scatter(
            section_one[2].astype(jnp.bfloat16), "grp", scatter_dimension=0, tiled=True
        ).astype(jnp.float32),
        lax.psum_scatter(
            section_one[3].astype(jnp.bfloat16), "grp", scatter_dimension=0, tiled=True
        ).astype(jnp.float32),
        lax.psum_scatter(
            section_one[4].astype(jnp.bfloat16), "grp", scatter_dimension=0, tiled=True
        ).astype(jnp.float32),
        lax.psum_scatter(
            section_one[5].astype(jnp.bfloat16), "grp", scatter_dimension=0, tiled=True
        ).astype(jnp.float32),
        lax.psum_scatter(
            section_one[6].astype(jnp.bfloat16), "grp", scatter_dimension=1, tiled=True
        ).astype(jnp.float32),
        lax.psum_scatter(
            section_one[7].astype(jnp.bfloat16), "grp", scatter_dimension=0, tiled=True
        ).astype(jnp.float32),
        lax.psum_scatter(
            section_one[8].astype(jnp.bfloat16), "grp", scatter_dimension=0, tiled=True
        ).astype(jnp.float32),
        lax.psum_scatter(
            section_one[9].astype(jnp.bfloat16), "grp", scatter_dimension=0, tiled=True
        ).astype(jnp.float32),
        lax.psum_scatter(
            section_one[10].astype(jnp.bfloat16), "grp", scatter_dimension=0, tiled=True
        ).astype(jnp.float32),
        lax.psum_scatter(
            section_one[11].astype(jnp.bfloat16), "grp", scatter_dimension=0, tiled=True
        ).astype(jnp.float32),
        lax.psum_scatter(
            section_one[12].astype(jnp.bfloat16), "grp", scatter_dimension=0, tiled=True
        ).astype(jnp.float32),
        lax.psum_scatter(
            section_one[13].astype(jnp.bfloat16), "grp", scatter_dimension=1, tiled=True
        ).astype(jnp.float32),
    )
    reduced = tuple((join_axis(section_two[pos], grad_dims[pos]) for pos in range(14)))
    return (
        out_all,
        grad_all,
        reduced[0],
        reduced[1],
        reduced[2],
        reduced[3],
        reduced[4],
        reduced[5],
        reduced[6],
        reduced[7],
        reduced[8],
        reduced[9],
        reduced[10],
        reduced[11],
        reduced[12],
        reduced[13],
    )


def solution(mesh):
    return jax.shard_map(
        shards,
        mesh=mesh,
        in_specs=(
            P(("grp", "shard"), None, None),
            P(("grp", "shard"), None, None),
            P(),
            P(),
            P(("grp", "shard")),
            P(("grp", "shard"), None),
            P(("grp", "shard"), None),
            P(("grp", "shard"), None),
            P(("grp", "shard"), None),
            P(("grp", "shard"), None),
            P(None, ("grp", "shard")),
            P(("grp", "shard")),
            P(("grp", "shard")),
            P(("grp", "shard"), None),
            P(("grp", "shard")),
            P(("grp", "shard"), None),
            P(("grp", "shard"), None),
            P(None, ("grp", "shard")),
        ),
        out_specs=(
            P(("grp", "shard"), None, None),
            P(("grp", "shard"), None, None),
            P(("grp", "shard")),
            P(("grp", "shard"), None),
            P(("grp", "shard"), None),
            P(("grp", "shard"), None),
            P(("grp", "shard"), None),
            P(("grp", "shard"), None),
            P(None, ("grp", "shard")),
            P(("grp", "shard")),
            P(("grp", "shard")),
            P(("grp", "shard"), None),
            P(("grp", "shard")),
            P(("grp", "shard"), None),
            P(("grp", "shard"), None),
            P(None, ("grp", "shard")),
        ),
        check_vma=False,
    )
```

profile of v0, /device:TPU:0, one launch (start us, length us, event | category | flops | bytes accessed | tf_op | source)
XLA Modules:
  0.0 1473.2 jit_solution(17731121891177173314)
XLA Ops:
  36.6 55.9 %all-reduce.11 = (bf16[1024]{0:T(1024)(128)(2,1)S(1)}, bf16[512]{0:T(512)(128)(2,1)S(1)}, bf16[256]{0:T(256)(128)(2,1)S(1)}, bf16[1024]{0:T(1024)(128)(2,1)S(1)}) all-reduce(bf16[1024]{0:T(1024)(128)(2,1)S(1)} %dynamic-update-slice, bf16[512]{0:T(512)(128)(2,1)S(1)} %dynamic-update-slice.1, ...), channel_id=1, replica_groups=mesh['grp'=4,'shard'=8] {'grp','shard'}, use_global_device_ids=true, to_apply=%add.2 | all-reduce | flops 2816 | bytes 11264
  108.2 60.5 %all-gather = bf16[32,32,16]{1,2,0:T(8,128)(2,1)S(1)} all-gather(bf16[1,32,16]{1,2,0:T(8,128)(2,1)S(1)} %bitcast.461), channel_id=1, replica_groups=mesh['grp'=4,'shard'=8] {'grp','shard'}, dimensions={0}, use_global_device_ids=true | all-gather | bytes 33792 | tf_op jit(solution)/shard_map/all_gather | solution.py:302
  177.6 64.0 %all_gather.60 = bf16[16,512]{0,1:T(8,128)(2,1)S(1)} all-gather(bf16[16,16]{0,1:T(8,128)(2,1)S(1)} %copy.177), channel_id=1, replica_groups=mesh['grp'=4,'shard'=8] {'grp','shard'}, dimensions={1}, use_global_device_ids=true | all-gather | bytes 16896 | tf_op jit(solution)/shard_map/all_gather | solution.py:303
  291.4 18.7 %all-to-all-done.4 = bf16[4,192,1024]{2,1,0:T(8,128)(2,1)} async-done(((bf16[4,192,1024]{2,1,0:T(8,128)(2,1)}), bf16[4,192,1024]{2,1,0:T(8,128)(2,1)}, u32[]{:S(2)}, u32[]{:S(2)}) %all-to-all-start.4) | async-done | bytes 1572896 | tf_op jit(solution)/shard_map/all_to_all | solution.py:347
  330.0 21.7 %while.65 = (s32[]{:T(128)}, f32[4,128,256]{2,1,0:T(8,128)S(1)}, f32[4,4,128,256]{3,2,1,0:T(8,128)}, f32[4,4,128]{2,1,0:T(4,128)}, pred[4]{0:T(512)(128)(4,1)}, ...) while((s32[]{:T(128)}, f32[4,128,256]{2,1,0:T(8,128)S(1)}, ...), condition=%wide.region_27.34_spmd.clone, body=%wide.region_26.33_spmd.clone.sunk | while | flops 786435 | bytes 2628219 | solution.py:144
  365.3 21.2 %while.64 = (s32[]{:T(128)}, f32[4,128,256]{2,1,0:T(8,128)S(1)}, f32[4,4,128,256]{3,2,1,0:T(8,128)}, f32[4,4,128]{2,1,0:T(4,128)}, pred[4]{0:T(512)(128)(4,1)}, ...) while((s32[]{:T(128)}, f32[4,128,256]{2,1,0:T(8,128)S(1)}, ...), condition=%wide.region_12.17_spmd.clone, body=%wide.region_11.16_spmd.clone.sunk | while | flops 786435 | bytes 2628219 | solution.py:144
  404.1 27.1 %all-gather.20.cloned.1.call-done = bf16[1024,2816]{1,0:T(8,128)(2,1)} async-done(((bf16[32,2816]{1,0:T(8,128)(2,1)}), bf16[1024,2816]{1,0:T(8,128)(2,1)}) %all-gather.20.cloned.1.call-update) | async-done | bytes 5767184 | tf_op jit(solution)/shard_map/all_gather | solution.py:308
  437.2 63.2 %all-gather.22.cloned.1.call-done = bf16[1024,2816]{1,0:T(8,128)(2,1)} async-done(((bf16[32,2816]{1,0:T(8,128)(2,1)}), bf16[1024,2816]{1,0:T(8,128)(2,1)}) %all-gather.22.cloned.1.call-update) | async-done | bytes 5767184 | tf_op jit(solution)/shard_map/all_gather | solution.py:309
  506.2 63.2 %all-gather.24.cloned.1.call-done = bf16[2816,1024]{0,1:T(8,128)(2,1)} async-done(((bf16[2816,32]{0,1:T(8,128)(2,1)}), bf16[2816,1024]{0,1:T(8,128)(2,1)}) %all-gather.24.cloned.1.call-update) | async-done | bytes 5767184 | tf_op jit(solution)/shard_map/all_gather | solution.py:310
  751.2 31.4 %reduce-scatter.35.cloned.1.call-done = bf16[4,32,512]{2,1,0:T(8,128)(2,1)} async-done(((bf16[4,256,512]{2,1,0:T(8,128)(2,1)}), bf16[4,32,512]{2,1,0:T(8,128)(2,1)}) %reduce-scatter.35.cloned.1.call-update) | async-done | bytes 131088 | tf_op jit(solution)/shard_map/reduce_scatter | solution.py:381
  792.8 28.9 %reduce-scatter.39.cloned.1.call-done = bf16[4,32,512]{2,1,0:T(8,128)(2,1)} async-done(((bf16[4,256,512]{2,1,0:T(8,128)(2,1)}), bf16[4,32,512]{2,1,0:T(8,128)(2,1)}) %reduce-scatter.39.cloned.1.call-update) | async-done | bytes 131088 | tf_op jit(solution)/shard_map/reduce_scatter | solution.py:384
  821.9 44.4 %reduce-scatter.43.cloned.1.call-done = bf16[4,32,1024]{2,1,0:T(8,128)(2,1)} async-done(((bf16[4,256,1024]{2,1,0:T(8,128)(2,1)}), bf16[4,32,1024]{2,1,0:T(8,128)(2,1)}) %reduce-scatter.43.cloned.1.call-update) | async-done | bytes 262160 | tf_op jit(solution)/shard_map/reduce_scatter | solution.py:387
  872.5 38.5 %reduce-scatter.47.cloned.1.call-done = bf16[4,32,1024]{2,1,0:T(8,128)(2,1)} async-done(((bf16[4,256,1024]{2,1,0:T(8,128)(2,1)}), bf16[4,32,1024]{2,1,0:T(8,128)(2,1)}) %reduce-scatter.47.cloned.1.call-update) | async-done | bytes 262160 | tf_op jit(solution)/shard_map/reduce_scatter | solution.py:390
  938.2 41.5 %all_to_all.40 = bf16[4,192,1024]{2,1,0:T(8,128)(2,1)} all-to-all(bf16[4,192,1024]{2,1,0:T(8,128)(2,1)S(1)} %get-tuple-element.669), channel_id=1, replica_groups=mesh['grp'=4,'shard'=8] {'grp'}, dimensions={0} | all-to-all | bytes 3145728 | tf_op jit(solution)/shard_map/all_to_all | solution.py:369
  999.4 21.6 %all-to-all-done.3 = bf16[4,192,1024]{2,1,0:T(8,128)(2,1)} async-done(((bf16[4,192,1024]{2,1,0:T(8,128)(2,1)}), bf16[4,192,1024]{2,1,0:T(8,128)(2,1)}, u32[]{:S(2)}, u32[]{:S(2)}) %all-to-all-start.3) | async-done | bytes 1572896 | tf_op jit(solution)/shard_map/all_to_all | solution.py:368
  1025.4 35.6 %all-to-all-done.5 = bf16[4,192,1024]{2,1,0:T(8,128)(2,1)S(1)} async-done(((bf16[4,192,1024]{2,1,0:T(8,128)(2,1)}), bf16[4,192,1024]{2,1,0:T(8,128)(2,1)S(1)}, u32[]{:S(2)}, u32[]{:S(2)}) %all-to-all-start.5) | async-done | bytes 1572896 | tf_op jit(solution)/shard_map/all_to_all | solution.py:369
  1090.6 36.0 %reduce-scatter.79.cloned.1.call-done = bf16[32,4]{1,0:T(8,128)(2,1)} async-done(((bf16[256,4]{1,0:T(8,128)(2,1)}), bf16[32,4]{1,0:T(8,128)(2,1)}) %reduce-scatter.79.cloned.1.call-update) | async-done | bytes 272
  1189.3 59.4 %reduce-scatter.63.cloned.1.call-done = bf16[4,32,2816]{2,1,0:T(8,128)(2,1)} async-done(((bf16[4,256,2816]{2,1,0:T(8,128)(2,1)}), bf16[4,32,2816]{2,1,0:T(8,128)(2,1)}) %reduce-scatter.63.cloned.1.call-update) | async-done | bytes 720912 | tf_op jit(solution)/shard_map/reduce_scatter | solution.py:414
  1248.8 21.3 %reduce-scatter.41.cloned.1.call-done = bf16[1,32,512]{2,1,0:T(8,128)(2,1)} async-done(((bf16[4,32,512]{2,1,0:T(8,128)(2,1)}), bf16[1,32,512]{2,1,0:T(8,128)(2,1)}) %reduce-scatter.41.cloned.1.call-update) | async-done | bytes 32784 | tf_op jit(solution)/shard_map/reduce_scatter | solution.py:428
  1311.9 59.1 %reduce-scatter.67.cloned.1.call-done = bf16[2816,4,32]{0,2,1:T(8,128)(2,1)} async-done(((bf16[2816,4,256]{0,2,1:T(8,128)(2,1)}), bf16[2816,4,32]{0,2,1:T(8,128)(2,1)}) %reduce-scatter.67.cloned.1.call-update) | async-done | bytes 720912 | tf_op jit(solution)/shard_map/reduce_scatter | solution.py:417
  1371.0 21.9 %reduce-scatter.57.cloned.1.call-done = bf16[1,32,1024]{2,1,0:T(8,128)(2,1)} async-done(((bf16[4,32,1024]{2,1,0:T(8,128)(2,1)}), bf16[1,32,1024]{2,1,0:T(8,128)(2,1)}) %reduce-scatter.57.cloned.1.call-update) | async-done | bytes 65552 | tf_op jit(solution)/shard_map/reduce_scatter | solution.py:449
  1394.4 22.0 %reduce-scatter.61.cloned.1.call-done = bf16[1,32,2816]{2,1,0:T(8,128)(2,1)} async-done(((bf16[4,32,2816]{2,1,0:T(8,128)(2,1)}), bf16[1,32,2816]{2,1,0:T(8,128)(2,1)}) %reduce-scatter.61.cloned.1.call-update) | async-done | bytes 180240 | tf_op jit(solution)/shard_map/reduce_scatter | solution.py:455
  1418.1 22.1 %reduce-scatter.65.cloned.1.call-done = bf16[1,32,2816]{2,1,0:T(8,128)(2,1)} async-done(((bf16[4,32,2816]{2,1,0:T(8,128)(2,1)}), bf16[1,32,2816]{2,1,0:T(8,128)(2,1)}) %reduce-scatter.65.cloned.1.call-update) | async-done | bytes 180240 | tf_op jit(solution)/shard_map/reduce_scatter | solution.py:458
  1441.9 22.4 %reduce-scatter.69.cloned.1.call-done = bf16[2816,1,32]{0,2,1:T(8,128)(2,1)} async-done(((bf16[2816,4,32]{0,2,1:T(8,128)(2,1)}), bf16[2816,1,32]{0,2,1:T(8,128)(2,1)}) %reduce-scatter.69.cloned.1.call-update) | async-done | bytes 180240 | tf_op jit(solution)/shard_map/reduce_scatter | solution.py:461
  (871 shorter events, 625.9 us)
Async XLA Ops:
  7.9 247.8 %all-gather.12.cloned.1.call-start = ((), (), s32[]{:S(2)}) async-start(), calls=%async_computation.32 | async-start | bytes 1081344 | tf_op jit(solution)/shard_map/all_gather | solution.py:298
  8.7 311.5 %all-gather.10.cloned.1.call-start = ((), (), s32[]{:S(2)}) async-start(), calls=%async_computation.31 | async-start | bytes 2162688 | tf_op jit(solution)/shard_map/all_gather | solution.py:300
  9.4 384.7 %all-gather.16.cloned.1.call-start = ((), (), s32[]{:S(2)}) async-start(), calls=%async_computation.34 | async-start | bytes 2162688 | tf_op jit(solution)/shard_map/all_gather | solution.py:301
  10.0 388.5 %all-gather.18.cloned.1.call-start = ((), (), s32[]{:S(2)}) async-start(), calls=%async_computation.35 | async-start | bytes 2162688 | tf_op jit(solution)/shard_map/all_gather | solution.py:306
  10.6 420.7 %all-gather.20.cloned.1.call-start = ((), (), s32[]{:S(2)}) async-start(), calls=%async_computation.36 | async-start | bytes 5947392 | tf_op jit(solution)/shard_map/all_gather | solution.py:308
  11.1 489.2 %all-gather.22.cloned.1.call-start = ((), (), s32[]{:S(2)}) async-start(), calls=%async_computation.37 | async-start | bytes 5947392 | tf_op jit(solution)/shard_map/all_gather | solution.py:309
  32.7 536.7 %all-gather.24.cloned.1.call-start = ((), (), s32[]{:S(2)}) async-start(), calls=%async_computation.38 | async-start | bytes 5947392 | tf_op jit(solution)/shard_map/all_gather | solution.py:310
  266.0 457.7 %reduce-scatter.75.cloned.1.call-start = ((), (), s32[]{:S(2)}) async-start(), calls=%async_computation.59 | async-start | bytes 36864
  697.4 327.3 %reduce-scatter.55.cloned.1.call-start = ((), (), s32[]{:S(2)}) async-start(), calls=%async_computation.49 | async-start | bytes 2359296 | tf_op jit(solution)/shard_map/reduce_scatter | solution.py:405
  701.6 366.0 %reduce-scatter.59.cloned.1.call-start = ((), (), s32[]{:S(2)}) async-start(), calls=%async_computation.51 | async-start | bytes 6488064 | tf_op jit(solution)/shard_map/reduce_scatter | solution.py:411
  709.0 371.4 %reduce-scatter.77.cloned.1.call-start = ((), (), s32[]{:S(2)}) async-start(), calls=%async_computation.60 | async-start | bytes 36864
  721.9 367.9 %reduce-scatter.71.cloned.1.call-start = ((), (), s32[]{:S(2)}) async-start(), calls=%async_computation.57 | async-start | bytes 73728
  722.8 403.8 %reduce-scatter.79.cloned.1.call-start = ((), (), s32[]{:S(2)}) async-start(), calls=%async_computation.61 | async-start | bytes 73728
  723.7 424.6 %reduce-scatter.53.cloned.1.call-start = ((), (), s32[]{:S(2)}) async-start(), calls=%async_computation.48 | async-start | bytes 20480 | tf_op jit(solution)/shard_map/reduce_scatter | solution.py:440
  725.2 443.0 %reduce-scatter.51.cloned.1.call-start = ((), (), s32[]{:S(2)}) async-start(), calls=%async_computation.47 | async-start | bytes 20480 | tf_op jit(solution)/shard_map/reduce_scatter | solution.py:437
  744.9 443.0 %reduce-scatter.37.cloned.1.call-start = ((), (), s32[]{:S(2)}) async-start(), calls=%async_computation.40 | async-start | bytes 163840 | tf_op jit(solution)/shard_map/reduce_scatter | solution.py:425
  782.7 466.0 %reduce-scatter.63.cloned.1.call-start = ((), (), s32[]{:S(2)}) async-start(), calls=%async_computation.53 | async-start | bytes 6488064 | tf_op jit(solution)/shard_map/reduce_scatter | solution.py:414
  791.8 478.3 %reduce-scatter.41.cloned.1.call-start = ((), (), s32[]{:S(2)}) async-start(), calls=%async_computation.42 | async-start | bytes 163840 | tf_op jit(solution)/shard_map/reduce_scatter | solution.py:428
  821.8 468.5 %reduce-scatter.45.cloned.1.call-start = ((), (), s32[]{:S(2)}) async-start(), calls=%async_computation.44 | async-start | bytes 327680 | tf_op jit(solution)/shard_map/reduce_scatter | solution.py:431
  866.3 444.1 %reduce-scatter.49.cloned.1.call-start = ((), (), s32[]{:S(2)}) async-start(), calls=%async_computation.46 | async-start | bytes 327680 | tf_op jit(solution)/shard_map/reduce_scatter | solution.py:434
  911.0 460.0 %reduce-scatter.67.cloned.1.call-start = ((), (), s32[]{:S(2)}) async-start(), calls=%async_computation.55 | async-start | bytes 6488064 | tf_op jit(solution)/shard_map/reduce_scatter | solution.py:417
  1024.6 368.3 %reduce-scatter.57.cloned.1.call-start = ((), (), s32[]{:S(2)}) async-start(), calls=%async_computation.50 | async-start | bytes 327680 | tf_op jit(solution)/shard_map/reduce_scatter | solution.py:449
  1065.5 350.9 %reduce-scatter.61.cloned.1.call-start = ((), (), s32[]{:S(2)}) async-start(), calls=%async_computation.52 | async-start | bytes 901120 | tf_op jit(solution)/shard_map/reduce_scatter | solution.py:455
  1067.6 372.6 %reduce-scatter.65.cloned.1.call-start = ((), (), s32[]{:S(2)}) async-start(), calls=%async_computation.54 | async-start | bytes 901120 | tf_op jit(solution)/shard_map/reduce_scatter | solution.py:458
  (217 other events, 4500.8 us)
Sparse Core Ops, SparseCore 0:
  10.9 70.8 all-gather.13
  84.6 70.3 all-gather.11
  157.9 71.6 all-gather.9
  232.2 70.9 all-gather.15
  306.0 56.3 all-gather.17
  365.1 66.1 all-gather.19
  434.1 66.2 all-gather.21
  503.2 66.2 all-gather.23
  676.2 30.2 reduce-scatter.74
  710.1 33.2 reduce-scatter.72
  746.6 36.0 reduce-scatter.34
  785.7 35.9 reduce-scatter.38
  825.0 41.1 reduce-scatter.42
  869.7 41.2 reduce-scatter.46
  914.1 41.2 reduce-scatter.54
  959.1 59.0 reduce-scatter.58
  1021.5 31.2 reduce-scatter.76
  1056.6 33.2 reduce-scatter.70
  1093.4 33.2 reduce-scatter.78
  1191.4 57.2 reduce-scatter.62
  1313.6 57.2 reduce-scatter.66
  1395.2 21.1 reduce-scatter.60
  1418.6 21.5 reduce-scatter.64
  1442.5 21.7 reduce-scatter.68
  (7 shorter events, 127.4 us)
where the time goes:
time: 1490 us; the launch traced here: 1470 us
  waiting for transfers between devices  739 us (50%)
  blocking collectives  246 us (17%)
  matrix products  177 us (12%)
  local copies, waits for them, and re-layouts  146 us (10%)
  other arithmetic  107 us (7%)
  starting transfers between devices  39 us (3%)
  between operations  18.3 us (1%)
    unnamed x3, blocking collectives  80.2 us
    unnamed x36, waiting for transfers between devices  68.9 us
    all_gather x1, blocking collectives, shards(): lax.all_gather(w_forget, ('grp', 'shard'), axis=1, tiled=True)  64 us
    all_gather x1, waiting for transfers between devices, shards(): lax.all_gather(w_down, ('grp', 'shard'), axis=1, tiled=True)  63.2 us
    all_gather x1, waiting for transfers between devices, shards(): lax.all_gather(w_up, ('grp', 'shard'), axis=0, tiled=True)  63.2 us
    all_gather x1, blocking collectives, shards(): lax.all_gather(w_lowrank, ('grp', 'shard'), axis=0, tiled=True)  60.5 us
    reduce_scatter x1, waiting for transfers between devices, shards(): lax.psum_scatter(split_grads[12].astype(jnp.bfloat16), 'shard', scatter_d...  59.4 us
    reduce_scatter x1, waiting for transfers between devices, shards(): lax.psum_scatter(split_grads[13].astype(jnp.bfloat16), 'shard', scatter_d...  59.1 us
  transfers between devices with their start and end apart: 38, of which 25 were waited for; matrix products, arithmetic and copies ran while one was open for 21% of the time, Pallas kernels for 0%

commit v1 on v0

v1 whole, which is shorter than its diff:
```python
import jax
import jax.numpy as jnp
from jax import lax
from jax.sharding import PartitionSpec as P

D = 1024
HEADS = 4
BLOCK = 64


EPS = 1e-05
HEAD_EPS = 1.0


def matmul(left_mat, right_mat):
    return jnp.dot(left_mat, right_mat, preferred_element_type=jnp.float32)


def rows_contract(left_mat, right_mat):
    return lax.dot_general(
        left_mat, right_mat, (((0,), (0,)), ((), ())), preferred_element_type=jnp.float32
    )


def right_transpose(left_mat, right_mat):
    return lax.dot_general(
        left_mat, right_mat, (((1,), (1,)), ((), ())), preferred_element_type=jnp.float32
    )


def scaled_rows(rows_in, gain_vec):
    return rows_in * lax.rsqrt(jnp.mean(rows_in * rows_in, axis=-1, keepdims=True) + EPS) * gain_vec


def head_rows(rows_in, gain_vec):
    return (
        rows_in
        * lax.rsqrt(jnp.mean(rows_in * rows_in, axis=-1, keepdims=True) + HEAD_EPS)
        * gain_vec
    )


def forget_rate(logits):
    return jax.nn.log_sigmoid(logits) / 16.0


def swiglu_core(pre_gate, pre_up):
    return jax.nn.silu(pre_gate) * pre_up


def head_gate(mixed_out, gate_out, head_gain):
    normed = head_rows(mixed_out, head_gain)
    active = gate_out * jax.nn.sigmoid(gate_out)
    return normed.reshape(active.shape) * active


def block_gates(queries, key_rows, forget):
    running = jnp.cumsum(forget, axis=1)
    tail_sum = running[:, -1:]
    q_gate = queries * queries.shape[-1] ** (-0.5) * jnp.exp(running)
    k_back = key_rows * jnp.exp(-running)
    k_tail = key_rows * jnp.exp(tail_sum - running)
    return (q_gate, k_back, k_tail, jnp.exp(tail_sum[:, 0]))


def layer_pass(weights, rows_in, back_in, seq_count):
    (
        g_attn,
        w_query,
        w_key,
        w_value,
        w_outgate,
        w_lowrank,
        w_forget,
        b_forget,
        g_head,
        w_output,
        g_ffn,
        w_gate,
        w_up,
        w_down,
    ) = weights
    row_count = rows_in.shape[0]
    blocks = row_count // BLOCK
    key_dim = w_query.shape[1] // HEADS
    val_dim = w_value.shape[1] // HEADS
    key_shape = (blocks, BLOCK, HEADS, key_dim)
    val_shape = (blocks, BLOCK, HEADS, val_dim)
    flat_rows = rows_in.astype(jnp.float32)
    norm_one, pull_one = jax.vjp(scaled_rows, flat_rows, g_attn.astype(jnp.float32))
    xn_one = norm_one.astype(jnp.bfloat16)
    queries = matmul(xn_one, w_query)
    key_rows = matmul(xn_one, w_key)
    values = matmul(xn_one, w_value).astype(jnp.bfloat16)
    gate_out = matmul(xn_one, w_outgate)
    lowrank = matmul(xn_one, w_lowrank).astype(jnp.bfloat16)
    logits = matmul(lowrank, w_forget) + b_forget.astype(jnp.float32)
    forget, pull_forget = jax.vjp(forget_rate, logits)
    gate_vals, pull_gates = jax.vjp(
        block_gates,
        queries.reshape(key_shape),
        key_rows.reshape(key_shape),
        forget.reshape(key_shape),
    )
    q_gate = gate_vals[0].astype(jnp.bfloat16)
    k_back = gate_vals[1].astype(jnp.bfloat16)
    k_tail = gate_vals[2].astype(jnp.bfloat16)
    decays = gate_vals[3]
    val_blocks = values.reshape(val_shape)
    spot_ids = jnp.arange(BLOCK)
    causal = (spot_ids[:, None] >= spot_ids[None, :]).astype(jnp.float32)
    scores = jnp.einsum("cthd,cshd->chts", q_gate, k_back, preferred_element_type=jnp.float32)
    attn_probs = (scores * causal).astype(jnp.bfloat16)
    intra_out = jnp.einsum(
        "chts,cshe->cthe", attn_probs, val_blocks, preferred_element_type=jnp.float32
    )
    update = jnp.einsum("cthd,cthe->chde", k_tail, val_blocks, preferred_element_type=jnp.float32)

    per_seq = blocks // seq_count
    seq_blocks = (seq_count, per_seq) + update.shape[1:]
    upd_seq = update.reshape(seq_blocks)
    decay_seq = decays.reshape((seq_count, per_seq) + decays.shape[1:])
    carried = jnp.zeros_like(upd_seq[:, 0])
    before_list = []
    for idx in range(per_seq):
        before_list.append(carried)
        carried = decay_seq[:, idx][..., None] * carried + upd_seq[:, idx]
    before_seq = jnp.stack(before_list, axis=1)
    before_low = before_seq.reshape(update.shape).astype(jnp.bfloat16)
    inter_out = jnp.einsum(
        "cthd,chde->cthe", q_gate, before_low, preferred_element_type=jnp.float32
    )
    mixed_out = (intra_out + inter_out).reshape(row_count, HEADS, val_dim)
    gated_f, pull_head = jax.vjp(head_gate, mixed_out, gate_out, g_head.astype(jnp.float32))
    gated_out = gated_f.astype(jnp.bfloat16)
    resid_one = flat_rows + matmul(gated_out, w_output)
    norm_two, pull_two = jax.vjp(scaled_rows, resid_one, g_ffn.astype(jnp.float32))
    xn_two = norm_two.astype(jnp.bfloat16)
    pre_gate = matmul(xn_two, w_gate)
    pre_up = matmul(xn_two, w_up)
    hidden_f, pull_ffn = jax.vjp(swiglu_core, pre_gate, pre_up)
    hidden = hidden_f.astype(jnp.bfloat16)
    output = (resid_one + matmul(hidden, w_down)).astype(jnp.bfloat16)
    back_f = back_in.astype(jnp.float32)
    dw_down = rows_contract(hidden, back_in)
    d_hidden = right_transpose(back_in, w_down)
    d_pre_gate, d_pre_up = pull_ffn(d_hidden)
    d_gate_low = d_pre_gate.astype(jnp.bfloat16)
    d_up_low = d_pre_up.astype(jnp.bfloat16)
    dw_gate = rows_contract(xn_two, d_gate_low)
    dw_up = rows_contract(xn_two, d_up_low)
    d_norm_two = right_transpose(d_gate_low, w_gate) + right_transpose(d_up_low, w_up)
    d_resid_part, dg_ffn = pull_two(d_norm_two)
    d_resid = back_f + d_resid_part
    d_attn = d_resid.astype(jnp.bfloat16)
    dw_output = rows_contract(gated_out, d_attn)
    d_gated = right_transpose(d_attn, w_output)
    d_mixed_f, d_gate_out_f, dg_head = pull_head(d_gated)
    d_mixed = d_mixed_f.astype(jnp.bfloat16).reshape(val_shape)
    d_scores = jnp.einsum(
        "cthe,cshe->chts", d_mixed, val_blocks, preferred_element_type=jnp.float32
    )
    d_probs = (d_scores * causal).astype(jnp.bfloat16)
    d_q_gate = jnp.einsum(
        "chts,cshd->cthd", d_probs, k_back, preferred_element_type=jnp.float32
    ) + jnp.einsum("cthe,chde->cthd", d_mixed, before_low, preferred_element_type=jnp.float32)
    d_k_back = jnp.einsum("chts,cthd->cshd", d_probs, q_gate, preferred_element_type=jnp.float32)
    d_val_intra = jnp.einsum(
        "chts,cthe->cshe", attn_probs, d_mixed, preferred_element_type=jnp.float32
    )
    d_before = jnp.einsum("cthd,cthe->chde", q_gate, d_mixed, preferred_element_type=jnp.float32)

    d_before_seq = d_before.reshape(seq_blocks)
    d_after = jnp.zeros_like(upd_seq[:, 0])
    d_update_list = []
    d_decay_list = []
    for idx in reversed(range(per_seq)):
        d_update_list.append(d_after)
        d_decay_list.append(jnp.sum(d_after * before_seq[:, idx], axis=-1))
        d_after = d_before_seq[:, idx] + decay_seq[:, idx][..., None] * d_after
    d_update = jnp.stack(d_update_list[::-1], axis=1).reshape(update.shape)
    d_decays = jnp.stack(d_decay_list[::-1], axis=1).reshape(decays.shape)
    d_update_low = d_update.astype(jnp.bfloat16)
    d_k_tail = jnp.einsum(
        "cthe,chde->cthd", val_blocks, d_update_low, preferred_element_type=jnp.float32
    )
    d_values = (
        (
            d_val_intra
            + jnp.einsum(
                "cthd,chde->cthe", k_tail, d_update_low, preferred_element_type=jnp.float32
            )
        )
        .reshape(row_count, -1)
        .astype(jnp.bfloat16)
    )
    d_query_f, d_key_f, d_forget = pull_gates((d_q_gate, d_k_back, d_k_tail, d_decays))
    d_queries = d_query_f.reshape(row_count, -1).astype(jnp.bfloat16)
    d_keys = d_key_f.reshape(row_count, -1).astype(jnp.bfloat16)
    (d_logits,) = pull_forget(d_forget.reshape(row_count, -1))
    db_forget = jnp.sum(d_logits, axis=0)
    d_logit_low = d_logits.astype(jnp.bfloat16)
    dw_forget = rows_contract(lowrank, d_logit_low)
    d_lowrank = right_transpose(d_logit_low, w_forget).astype(jnp.bfloat16)
    d_gate_out = d_gate_out_f.astype(jnp.bfloat16)
    dw_query = rows_contract(xn_one, d_queries)
    dw_key = rows_contract(xn_one, d_keys)
    dw_value = rows_contract(xn_one, d_values)
    dw_outgate = rows_contract(xn_one, d_gate_out)
    dw_lowrank = rows_contract(xn_one, d_lowrank)
    d_norm_one = (
        right_transpose(d_queries, w_query)
        + right_transpose(d_keys, w_key)
        + right_transpose(d_values, w_value)
        + right_transpose(d_gate_out, w_outgate)
        + right_transpose(d_lowrank, w_lowrank)
    )
    d_flat, dg_attn = pull_one(d_norm_one)
    grad_rows = (d_resid + d_flat).astype(jnp.bfloat16)
    grads = (
        dg_attn,
        dw_query,
        dw_key,
        dw_value,
        dw_outgate,
        dw_lowrank,
        dw_forget,
        db_forget,
        dg_head,
        dw_output,
        dg_ffn,
        dw_gate,
        dw_up,
        dw_down,
    )
    return (output, grad_rows, grads)


def shards(
    inputs,
    cotangent,
    lengths,
    dealing,
    g_attn,
    w_query,
    w_key,
    w_value,
    w_outgate,
    w_lowrank,
    w_forget,
    b_forget,
    g_head,
    w_output,
    g_ffn,
    w_gate,
    w_up,
    w_down,
):
    axes = ("grp", "shard")
    shard_count = lax.axis_size("shard")
    self_index = lax.axis_index("grp") * shard_count + lax.axis_index("shard")
    seq_dev, max_len, _ = inputs.shape
    own_given = self_index * seq_dev + jnp.arange(seq_dev, dtype=jnp.int32)
    own_len = jnp.sum(jnp.where(dealing[None, :] == own_given[:, None], lengths[None, :], 0), axis=1)
    live = jnp.arange(max_len, dtype=jnp.int32)[None, :] < own_len[:, None]
    zero_low = jnp.zeros((), jnp.bfloat16)
    rows_in = jnp.where(live[..., None], inputs, zero_low).reshape(seq_dev * max_len, D)
    back_in = jnp.where(live[..., None], cotangent, zero_low).reshape(seq_dev * max_len, D)
    shard_weights = (
        g_attn,
        w_query,
        w_key,
        w_value,
        w_outgate,
        w_lowrank,
        w_forget,
        b_forget,
        g_head,
        w_output,
        g_ffn,
        w_gate,
        w_up,
        w_down,
    )
    grad_dims = (0, 0, 0, 0, 0, 0, 1, 0, 0, 0, 0, 0, 0, 1)
    gathered = tuple(
        lax.all_gather(weight, axes, axis=dim, tiled=True)
        for weight, dim in zip(shard_weights, grad_dims)
    )
    out_rows, grad_rows, grads = layer_pass(gathered, rows_in, back_in, seq_dev)
    reduced = tuple(
        lax.psum_scatter(
            grad.astype(jnp.bfloat16), axes, scatter_dimension=dim, tiled=True
        ).astype(jnp.float32)
        for grad, dim in zip(grads, grad_dims)
    )
    return (out_rows.reshape(inputs.shape), grad_rows.reshape(inputs.shape)) + reduced


def solution(mesh):
    return jax.shard_map(
        shards,
        mesh=mesh,
        in_specs=(
            P(("grp", "shard"), None, None),
            P(("grp", "shard"), None, None),
            P(),
            P(),
            P(("grp", "shard")),
            P(("grp", "shard"), None),
            P(("grp", "shard"), None),
            P(("grp", "shard"), None),
            P(("grp", "shard"), None),
            P(("grp", "shard"), None),
            P(None, ("grp", "shard")),
            P(("grp", "shard")),
            P(("grp", "shard")),
            P(("grp", "shard"), None),
            P(("grp", "shard")),
            P(("grp", "shard"), None),
            P(("grp", "shard"), None),
            P(None, ("grp", "shard")),
        ),
        out_specs=(
            P(("grp", "shard"), None, None),
            P(("grp", "shard"), None, None),
            P(("grp", "shard")),
            P(("grp", "shard"), None),
            P(("grp", "shard"), None),
            P(("grp", "shard"), None),
            P(("grp", "shard"), None),
            P(("grp", "shard"), None),
            P(None, ("grp", "shard")),
            P(("grp", "shard")),
            P(("grp", "shard")),
            P(("grp", "shard"), None),
            P(("grp", "shard")),
            P(("grp", "shard"), None),
            P(("grp", "shard"), None),
            P(None, ("grp", "shard")),
        ),
        check_vma=False,
    )
```

time: 1490 us -> 1960 us (1.32)
  waiting for transfers between devices: 739 us -> 1490 us
  blocking collectives: 246 us -> 160 us
  local copies, waits for them, and re-layouts: 146 us -> 66.5 us
  other arithmetic: 107 us -> 47.2 us
  starting transfers between devices: 39 us -> 1.1 us
    reduce_scatter x18 -> x8, waiting for transfers between devices: 440 us -> 1080 us  [shards(): lax.psum_scatter(grad.astype(jnp.bfloat16), axes, scatter_dimension=dim,...]
    all_gather x8, waiting for transfers between devices: 154 us -> 270 us  [shards(): lax.all_gather(weight, axes, axis=dim, tiled=True)]
    all_to_all x7 -> x0, waiting for transfers between devices: 75.9 us -> none  [the longest x1 35.6 us: shards(): lax.all_to_all(ret_grad, 'grp', split_axis=0, concat_axis=0, tiled=True)]
    unnamed x36 -> x20, waiting for transfers between devices: 68.9 us -> 136 us
    all_gather x2, blocking collectives: 124 us -> 77.7 us  [shards(): lax.all_gather(weight, axes, axis=dim, tiled=True)]
    gather x18 -> x0, local copies, waits for them, and re-layouts: 44.2 us -> none  [the longest x2 8.24 us: shards(): jnp.take(recv_back.reshape(-1, D), fetch_ids, axis=0)]
    all_to_all x1 -> x0, blocking collectives: 41.5 us -> none  [shards(): lax.all_to_all(ret_grad, 'grp', split_axis=0, concat_axis=0, tiled=True)]
    all_to_all x7 -> x0, starting transfers between devices: 37.2 us -> none  [the longest x2 13.5 us: shards(): lax.all_to_all(send_back, 'grp', split_axis=0, concat_axis=0, tiled=True)]
  transfers between devices with their start and end apart: 38 -> 18, of which waited for: 25 -> 16; matrix products, arithmetic and copies ran while one was open for 21% -> 10% of each run, Pallas kernels for 0% -> 0%
where the time goes in v1:
time: 1960 us; the launch traced here: 1950 us
  waiting for transfers between devices  1490 us (76%)
  matrix products  171 us (9%)
  blocking collectives  160 us (8%)
  local copies, waits for them, and re-layouts  66.5 us (3%)
  other arithmetic  47.2 us (2%)
    reduce_scatter x8, waiting for transfers between devices, shards(): lax.psum_scatter(grad.astype(jnp.bfloat16), axes, scatter_dimension=dim,...  1080 us
    all_gather x8, waiting for transfers between devices, shards(): lax.all_gather(weight, axes, axis=dim, tiled=True)  270 us
    unnamed x20, waiting for transfers between devices  136 us
    unnamed x2, blocking collectives  82.2 us
    all_gather x2, blocking collectives, shards(): lax.all_gather(weight, axes, axis=dim, tiled=True)  77.7 us
    dot_general x10, matrix products, matmul(): return jnp.dot(left_mat, right_mat, preferred_element_type=jnp.float32)  58.9 us
    dot_general x10, matrix products, right_transpose(): lax.dot_general(left_mat, right_mat, (((1,), (1,)), ((), ())), preferred_...  48.9 us
    dot_general x10, matrix products, rows_contract(): lax.dot_general(left_mat, right_mat, (((0,), (0,)), ((), ())), preferred_...  48.7 us
  transfers between devices with their start and end apart: 18, of which 16 were waited for; matrix products, arithmetic and copies ran while one was open for 10% of the time, Pallas kernels for 0%

profile of v1, /device:TPU:0, one launch (start us, length us, event | category | flops | bytes accessed | tf_op | source)
XLA Modules:
  0.0 1950.8 jit_solution(191389552123489193)
XLA Ops:
  16.1 42.1 %all-reduce.10 = (bf16[1024]{0:T(1024)(128)(2,1)S(1)}, bf16[512]{0:T(512)(128)(2,1)S(1)}, bf16[256]{0:T(256)(128)(2,1)S(1)}, bf16[1024]{0:T(1024)(128)(2,1)S(1)}) all-reduce(bf16[1024]{0:T(1024)(128)(2,1)S(1)} %dynamic-update-slice, bf16[512]{0:T(512)(128)(2,1)S(1)} %dynamic-update-slice.1, ...), channel_id=1, replica_groups=mesh['grp'=4,'shard'=8] {'grp','shard'}, use_global_device_ids=true, to_apply=%add.1 | all-reduce | flops 2816 | bytes 11264
  62.0 40.6 %all-gather = bf16[32,32,16]{1,2,0:T(8,128)(2,1)S(1)} all-gather(bf16[1,32,16]{1,2,0:T(8,128)(2,1)S(1)} %bitcast.296), channel_id=1, replica_groups=mesh['grp'=4,'shard'=8] {'grp','shard'}, dimensions={0}, use_global_device_ids=true | all-gather | bytes 33792 | tf_op jit(solution)/shard_map/all_gather | solution.py:287
  102.9 37.1 %all_gather.46 = bf16[16,512]{0,1:T(8,128)(2,1)S(1)} all-gather(bf16[16,16]{0,1:T(8,128)(2,1)S(1)} %copy.117), channel_id=1, replica_groups=mesh['grp'=4,'shard'=8] {'grp','shard'}, dimensions={1}, use_global_device_ids=true | all-gather | bytes 16896 | tf_op jit(solution)/shard_map/all_gather | solution.py:287
  168.7 12.6 all-gather.10.cloned.1.call-done
  208.1 31.2 %all-gather.16.cloned.1.call-done = bf16[1024,1024]{1,0:T(8,128)(2,1)} async-done(((bf16[32,1024]{1,0:T(8,128)(2,1)}), bf16[1024,1024]{1,0:T(8,128)(2,1)}) %all-gather.16.cloned.1.call-update) | async-done | bytes 2097168 | tf_op jit(solution)/shard_map/all_gather | solution.py:287
  248.5 48.8 %all-gather.18.cloned.1.call-done = bf16[1024,1024]{1,0:T(8,128)(2,1)} async-done(((bf16[32,1024]{1,0:T(8,128)(2,1)}), bf16[1024,1024]{1,0:T(8,128)(2,1)}) %all-gather.18.cloned.1.call-update) | async-done | bytes 2097168 | tf_op jit(solution)/shard_map/all_gather | solution.py:287
  304.8 61.3 %all-gather.20.cloned.1.call-done = bf16[1024,2816]{1,0:T(8,128)(2,1)} async-done(((bf16[32,2816]{1,0:T(8,128)(2,1)}), bf16[1024,2816]{1,0:T(8,128)(2,1)}) %all-gather.20.cloned.1.call-update) | async-done | bytes 5767184 | tf_op jit(solution)/shard_map/all_gather | solution.py:287
  366.1 11.2 fusion.81
  377.3 57.9 %all-gather.22.cloned.1.call-done = bf16[1024,2816]{1,0:T(8,128)(2,1)} async-done(((bf16[32,2816]{1,0:T(8,128)(2,1)}), bf16[1024,2816]{1,0:T(8,128)(2,1)}) %all-gather.22.cloned.1.call-update) | async-done | bytes 5767184 | tf_op jit(solution)/shard_map/all_gather | solution.py:287
  435.2 11.3 fusion.82
  446.5 57.8 %all-gather.24.cloned.1.call-done = bf16[2816,1024]{0,1:T(8,128)(2,1)} async-done(((bf16[2816,32]{0,1:T(8,128)(2,1)}), bf16[2816,1024]{0,1:T(8,128)(2,1)}) %all-gather.24.cloned.1.call-update) | async-done | bytes 5767184 | tf_op jit(solution)/shard_map/all_gather | solution.py:287
  504.3 16.1 multiply_convert_fusion
  520.4 11.8 fusion.83
  656.6 40.1 %all-reduce.9 = (bf16[1024]{0:T(1024)(128)(2,1)S(1)}, bf16[512]{0:T(512)(128)(2,1)S(1)}, bf16[256]{0:T(256)(128)(2,1)S(1)}, bf16[1024]{0:T(1024)(128)(2,1)S(1)}) all-reduce(bf16[1024]{0:T(1024)(128)(2,1)S(1)} %get-tuple-element.21, ...), channel_id=2, replica_groups=mesh['grp'=4,'shard'=8] {'grp','shard'}, use_global_device_ids=true, to_apply=%region_14.15.clone | all-reduce | flops 2816 | bytes 11264
  703.5 9.8 add_convert_fusion.1
  714.7 130.8 %reduce-scatter.31.cloned.1.call-done = bf16[32,16]{1,0:T(8,128)(2,1)} async-done(((bf16[1024,16]{1,0:T(8,128)(2,1)}), bf16[32,16]{1,0:T(8,128)(2,1)}) %reduce-scatter.31.cloned.1.call-update) | async-done | bytes 1040
  846.9 131.6 %reduce-scatter.15.cloned.1.call-done = bf16[32,512]{1,0:T(8,128)(2,1)} async-done(((bf16[1024,512]{1,0:T(8,128)(2,1)}), bf16[32,512]{1,0:T(8,128)(2,1)}) %reduce-scatter.15.cloned.1.call-update) | async-done | bytes 32784 | tf_op jit(solution)/shard_map/reduce_scatter | solution.py:292
  979.9 131.5 %reduce-scatter.17.cloned.1.call-done = bf16[32,512]{1,0:T(8,128)(2,1)} async-done(((bf16[1024,512]{1,0:T(8,128)(2,1)}), bf16[32,512]{1,0:T(8,128)(2,1)}) %reduce-scatter.17.cloned.1.call-update) | async-done | bytes 32784 | tf_op jit(solution)/shard_map/reduce_scatter | solution.py:292
  1112.8 133.4 %reduce-scatter.23.cloned.1.call-done = bf16[32,1024]{1,0:T(8,128)(2,1)} async-done(((bf16[1024,1024]{1,0:T(8,128)(2,1)}), bf16[32,1024]{1,0:T(8,128)(2,1)}) %reduce-scatter.23.cloned.1.call-update) | async-done | bytes 65552 | tf_op jit(solution)/shard_map/reduce_scatter | solution.py:292
  1247.7 133.3 %reduce-scatter.19.cloned.1.call-done = bf16[32,1024]{1,0:T(8,128)(2,1)} async-done(((bf16[1024,1024]{1,0:T(8,128)(2,1)}), bf16[32,1024]{1,0:T(8,128)(2,1)}) %reduce-scatter.19.cloned.1.call-update) | async-done | bytes 65552 | tf_op jit(solution)/shard_map/reduce_scatter | solution.py:292
  1382.6 133.3 %reduce-scatter.21.cloned.1.call-done = bf16[32,1024]{1,0:T(8,128)(2,1)} async-done(((bf16[1024,1024]{1,0:T(8,128)(2,1)}), bf16[32,1024]{1,0:T(8,128)(2,1)}) %reduce-scatter.21.cloned.1.call-update) | async-done | bytes 65552 | tf_op jit(solution)/shard_map/reduce_scatter | solution.py:292
  1517.3 140.4 %reduce-scatter.25.cloned.1.call-done = bf16[32,2816]{1,0:T(8,128)(2,1)} async-done(((bf16[1024,2816]{1,0:T(8,128)(2,1)}), bf16[32,2816]{1,0:T(8,128)(2,1)}) %reduce-scatter.25.cloned.1.call-update) | async-done | bytes 180240 | tf_op jit(solution)/shard_map/reduce_scatter | solution.py:292
  1659.5 140.3 %reduce-scatter.27.cloned.1.call-done = bf16[32,2816]{1,0:T(8,128)(2,1)} async-done(((bf16[1024,2816]{1,0:T(8,128)(2,1)}), bf16[32,2816]{1,0:T(8,128)(2,1)}) %reduce-scatter.27.cloned.1.call-update) | async-done | bytes 180240 | tf_op jit(solution)/shard_map/reduce_scatter | solution.py:292
  1801.5 140.5 %reduce-scatter.29.cloned.1.call-done = bf16[2816,32]{0,1:T(8,128)(2,1)} async-done(((bf16[2816,1024]{0,1:T(8,128)(2,1)}), bf16[2816,32]{0,1:T(8,128)(2,1)}) %reduce-scatter.29.cloned.1.call-update) | async-done | bytes 180240 | tf_op jit(solution)/shard_map/reduce_scatter | solution.py:292
  (330 shorter events, 230.5 us)
Async XLA Ops:
  7.2 54.8 %copy-start.69 = (bf16[32,16]{0,1:T(8,128)(2,1)S(1)}, bf16[32,16]{0,1:T(8,128)(2,1)}, u32[]{:S(2)}) copy-start(bf16[32,16]{0,1:T(8,128)(2,1)} %param.27) | copy-start | bytes 3076
  7.2 147.3 %all-gather.14.cloned.1.call-start = ((), (), s32[]{:S(2)}) async-start(), calls=%async_computation.12 | async-start | bytes 1081344 | tf_op jit(solution)/shard_map/all_gather | solution.py:287
  7.9 149.0 %all-gather.12.cloned.1.call-start = ((), (), s32[]{:S(2)}) async-start(), calls=%async_computation.11 | async-start | bytes 1081344 | tf_op jit(solution)/shard_map/all_gather | solution.py:287
  8.7 172.6 %all-gather.10.cloned.1.call-start = ((), (), s32[]{:S(2)}) async-start(), calls=%async_computation.10 | async-start | bytes 2162688 | tf_op jit(solution)/shard_map/all_gather | solution.py:287
  9.4 229.9 %all-gather.16.cloned.1.call-start = ((), (), s32[]{:S(2)}) async-start(), calls=%async_computation.13 | async-start | bytes 2162688 | tf_op jit(solution)/shard_map/all_gather | solution.py:287
  10.0 287.3 %all-gather.18.cloned.1.call-start = ((), (), s32[]{:S(2)}) async-start(), calls=%async_computation.14 | async-start | bytes 2162688 | tf_op jit(solution)/shard_map/all_gather | solution.py:287
  10.6 355.5 %all-gather.20.cloned.1.call-start = ((), (), s32[]{:S(2)}) async-start(), calls=%async_computation.15 | async-start | bytes 5947392 | tf_op jit(solution)/shard_map/all_gather | solution.py:287
  11.1 91.7 %copy-start.70 = (bf16[16,16]{1,0:T(8,128)(2,1)S(1)}, bf16[16,16]{1,0:T(8,128)(2,1)}, u32[]{:S(2)}) copy-start(bf16[16,16]{1,0:T(8,128)(2,1)} %param.28) | copy-start | bytes 1540
  11.2 424.1 %all-gather.22.cloned.1.call-start = ((), (), s32[]{:S(2)}) async-start(), calls=%async_computation.16 | async-start | bytes 5947392 | tf_op jit(solution)/shard_map/all_gather | solution.py:287
  11.9 492.4 %all-gather.24.cloned.1.call-start = ((), (), s32[]{:S(2)}) async-start(), calls=%async_computation.17 | async-start | bytes 5947392 | tf_op jit(solution)/shard_map/all_gather | solution.py:287
  12.7 700.7 %reduce-scatter.33.cloned.1.call-start = ((), (), s32[]{:S(2)}) async-start(), calls=%async_computation.27 | async-start | bytes 135168
  58.2 92.5 %copy-start.56 = (f32[1024]{0:T(1024)}, f32[1024]{0:T(1024)S(1)}, u32[]{:S(2)}) copy-start(f32[1024]{0:T(1024)S(1)} %convert_element_type.244) | copy-start | bytes 12292
  61.2 89.5 %copy-start = (bf16[4,192,1024]{2,1,0:T(8,128)(2,1)}, bf16[4,192,1024]{2,1,0:T(8,128)(2,1)S(1)}, u32[]{:S(2)}) copy-start(bf16[4,192,1024]{2,1,0:T(8,128)(2,1)S(1)} %get-tuple-element.40) | copy-start | bytes 4718596
  61.3 79.6 %copy-start.62 = (f32[768]{0:T(1024)}, f32[768]{0:T(1024)S(1)}, u32[]{:S(2)}) copy-start(f32[768]{0:T(1024)S(1)} %rsqrt.40) | copy-start | bytes 9220
  580.8 264.7 %reduce-scatter.31.cloned.1.call-start = ((), (), s32[]{:S(2)}) async-start(), calls=%async_computation.26 | async-start | bytes 270336
  585.1 393.4 %reduce-scatter.15.cloned.1.call-start = ((), (), s32[]{:S(2)}) async-start(), calls=%async_computation.18 | async-start | bytes 1081344 | tf_op jit(solution)/shard_map/reduce_scatter | solution.py:292
  588.7 522.7 %reduce-scatter.17.cloned.1.call-start = ((), (), s32[]{:S(2)}) async-start(), calls=%async_computation.19 | async-start | bytes 1081344 | tf_op jit(solution)/shard_map/reduce_scatter | solution.py:292
  594.9 651.3 %reduce-scatter.23.cloned.1.call-start = ((), (), s32[]{:S(2)}) async-start(), calls=%async_computation.22 | async-start | bytes 2162688 | tf_op jit(solution)/shard_map/reduce_scatter | solution.py:292
  600.7 780.4 %reduce-scatter.19.cloned.1.call-start = ((), (), s32[]{:S(2)}) async-start(), calls=%async_computation.20 | async-start | bytes 2162688 | tf_op jit(solution)/shard_map/reduce_scatter | solution.py:292
  609.7 906.1 %reduce-scatter.21.cloned.1.call-start = ((), (), s32[]{:S(2)}) async-start(), calls=%async_computation.21 | async-start | bytes 2162688 | tf_op jit(solution)/shard_map/reduce_scatter | solution.py:292
  615.7 1042.1 %reduce-scatter.25.cloned.1.call-start = ((), (), s32[]{:S(2)}) async-start(), calls=%async_computation.23 | async-start | bytes 5947392 | tf_op jit(solution)/shard_map/reduce_scatter | solution.py:292
  625.9 1173.9 %reduce-scatter.27.cloned.1.call-start = ((), (), s32[]{:S(2)}) async-start(), calls=%async_computation.24 | async-start | bytes 5947392 | tf_op jit(solution)/shard_map/reduce_scatter | solution.py:292
  635.0 1307.0 %reduce-scatter.29.cloned.1.call-start = ((), (), s32[]{:S(2)}) async-start(), calls=%async_computation.25 | async-start | bytes 5947392 | tf_op jit(solution)/shard_map/reduce_scatter | solution.py:292
  653.5 44.9 %copy-start.66 = (f32[768]{0:T(1024)S(1)}, f32[768]{0:T(1024)}, u32[]{:S(2)}) copy-start(f32[768]{0:T(1024)} %copy-done.65) | copy-start | bytes 9220
  (76 other events, 356.0 us)
Sparse Core Ops, SparseCore 0:
  10.9 56.5 all-gather.13
  70.3 52.7 all-gather.11
  126.0 55.2 all-gather.9
  184.0 55.2 all-gather.15
  242.0 55.2 all-gather.17
  299.9 66.1 all-gather.19
  368.9 66.2 all-gather.21
  438.0 66.2 all-gather.23
  581.0 132.3 reduce-scatter.32
  716.1 129.3 reduce-scatter.30
  847.8 130.6 reduce-scatter.14
  980.7 130.6 reduce-scatter.16
  1113.7 132.5 reduce-scatter.22
  1248.4 132.5 reduce-scatter.18
  1383.2 132.6 reduce-scatter.20
  1518.1 139.6 reduce-scatter.24
  1660.0 139.6 reduce-scatter.26
  1802.0 139.8 reduce-scatter.28

commit v2 on v1

--- a/solution.py
+++ b/solution.py
@@ -1,6 +1,8 @@
 import jax
 import jax.numpy as jnp
 from jax import lax
+from jax.experimental import pallas as pl
+from jax.experimental.pallas import tpu as pltpu
 from jax.sharding import PartitionSpec as P
 
 D = 1024
@@ -10,6 +12,16 @@
 
 EPS = 1e-05
 HEAD_EPS = 1.0
+
+MESH = pl.DeviceIdType.MESH
+DMA = pltpu.SemaphoreType.DMA
+GRP = 4
+SHARD = 8
+ROWS = 32
+WIDE = 768
+FF_CUT = 256
+SLOTS = 6
+MISC = 128
 
 
 def matmul(left_mat, right_mat):
@@ -236,7 +248,480 @@
     return (output, grad_rows, grads)
 
 
-def shards(
+def flip(index, bit):
+    return index + bit - 2 * bit * lax.rem(index // bit, 2)
+
+
+def remote(src, dst, send_sem, recv_sem, device):
+    return pltpu.make_async_remote_copy(
+        src_ref=src,
+        dst_ref=dst,
+        send_sem=send_sem,
+        recv_sem=recv_sem,
+        device_id=device,
+        device_id_type=MESH,
+    )
+
+
+def start_all(copies):
+    for copy in copies:
+        copy.start()
+
+
+def recv_all(copies):
+    for copy in copies:
+        copy.wait_recv()
+
+
+def sent_all(copies):
+    for copy in copies:
+        copy.wait_send()
+
+
+class Place:
+    def __init__(self):
+        self.z = lax.axis_index("grp")
+        self.s = lax.axis_index("shard")
+        self.sib = flip(self.s, 1)
+        self.xn = flip(self.s, 2)
+        self.yn = flip(self.s, 4)
+        self.dg = flip(self.xn, 4)
+        self.sets = [self.s, self.xn, self.yn, self.dg]
+        self.z_peers = [lax.rem(self.z + step, GRP) for step in range(1, GRP)]
+        self.z_from = [lax.rem(self.z + GRP - step, GRP) for step in range(1, GRP)]
+
+    def greet(self):
+        barrier = pltpu.get_barrier_semaphore()
+        peers = [(peer, self.s) for peer in self.z_peers]
+        peers += [(self.z, self.sib), (self.z, self.xn), (self.z, self.yn)]
+        for peer in peers:
+            pl.semaphore_signal(barrier, inc=1, device_id=peer, device_id_type=MESH)
+        return (barrier, len(peers))
+
+
+class Gather:
+    def __init__(self, place, src, full, sems):
+        self.p = place
+        self.src = src
+        self.full = full
+        (
+            self.ls,
+            self.zs,
+            self.zr,
+            self.xs,
+            self.xr,
+            self.ds,
+            self.dr,
+            self.ss,
+            self.sr,
+        ) = sems
+
+    def local(self, c):
+        p = self.p
+        return pltpu.make_async_copy(self.src.at[c], self.full.at[c, p.z, p.s], self.ls.at[c])
+
+    def line(self, c):
+        p = self.p
+        return [
+            remote(
+                self.src.at[c],
+                self.full.at[c, p.z, p.s],
+                self.zs.at[c, k],
+                self.zr.at[c, k],
+                (p.z_peers[k], p.s),
+            )
+            for k in range(GRP - 1)
+        ]
+
+    def line_in(self, c):
+        p = self.p
+        return [
+            remote(
+                self.src.at[c],
+                self.full.at[c, p.z_from[k], p.s],
+                self.zs.at[c, k],
+                self.zr.at[c, k],
+                (p.z_peers[k], p.s),
+            )
+            for k in range(GRP - 1)
+        ]
+
+    def moved(self, c, set_id, part, send, recv, k, device):
+        view = self.full.at[c, part, set_id]
+        return remote(view, view, send.at[c, k], recv.at[c, k], device)
+
+    def plane(self, c):
+        p = self.p
+        whole = pl.ds(0, GRP)
+        return [
+            self.moved(c, p.s, whole, self.xs, self.xr, 0, (p.z, p.xn)),
+            self.moved(c, p.s, whole, self.xs, self.xr, 1, (p.z, p.yn)),
+        ]
+
+    def plane_in(self, c):
+        p = self.p
+        whole = pl.ds(0, GRP)
+        return [
+            self.moved(c, p.xn, whole, self.xs, self.xr, 0, (p.z, p.xn)),
+            self.moved(c, p.yn, whole, self.xs, self.xr, 1, (p.z, p.yn)),
+        ]
+
+    def corner(self, c):
+        p = self.p
+        low, high = pl.ds(0, 2), pl.ds(2, 2)
+        return [
+            self.moved(c, p.xn, low, self.ds, self.dr, 0, (p.z, p.yn)),
+            self.moved(c, p.yn, high, self.ds, self.dr, 1, (p.z, p.xn)),
+        ]
+
+    def corner_in(self, c):
+        p = self.p
+        low, high = pl.ds(0, 2), pl.ds(2, 2)
+        return [
+            self.moved(c, p.dg, low, self.ds, self.dr, 0, (p.z, p.yn)),
+            self.moved(c, p.dg, high, self.ds, self.dr, 1, (p.z, p.xn)),
+        ]
+
+    def other(self, c, k):
+        p = self.p
+        return self.moved(c, p.sets[k], pl.ds(0, GRP), self.ss, self.sr, k, (p.z, p.sib))
+
+    def other_in(self, c):
+        p = self.p
+        return [
+            self.moved(c, flip(p.sets[k], 1), pl.ds(0, GRP), self.ss, self.sr, k, (p.z, p.sib))
+            for k in range(4)
+        ]
+
+    def step(self, t, chunks, ahead):
+        if t + ahead < chunks:
+            start_all(self.line(t + ahead))
+        if t < chunks:
+            self.local(t).wait()
+            recv_all(self.line_in(t))
+            start_all(self.plane(t))
+            self.other(t, 0).start()
+        if 0 <= t - 1 < chunks:
+            recv_all(self.plane_in(t - 1))
+            start_all(self.corner(t - 1))
+            self.other(t - 1, 1).start()
+            self.other(t - 1, 2).start()
+        if 0 <= t - 2 < chunks:
+            recv_all(self.corner_in(t - 2))
+            self.other(t - 2, 3).start()
+        if 0 <= t - 3 < chunks:
+            recv_all(self.other_in(t - 3))
+
+    def drain(self, c):
+        sent_all(self.line(c) + self.plane(c) + self.corner(c))
+        sent_all([self.other(c, k) for k in range(4)])
+
+
+def gather_sems(chunks):
+    counts = (3, 3, 2, 2, 2, 2, 4, 4)
+    return [DMA((chunks,))] + [DMA((chunks, count)) for count in counts]
+
+
+def gather_kernel(src, full, *sems):
+    chunks = src.shape[0]
+    place = Place()
+    barrier, greeted = place.greet()
+    gather = Gather(place, src, full, sems)
+    start_all([gather.local(c) for c in range(chunks)])
+    pl.semaphore_wait(barrier, greeted)
+    ahead = 3
+    for c in range(ahead):
+        start_all(gather.line(c))
+    for t in range(chunks + 3):
+        gather.step(t, chunks, ahead)
+    for c in range(chunks):
+        gather.drain(c)
+
+
+def gather_call(src):
+    chunks = src.shape[0]
+    return pl.pallas_call(
+        gather_kernel,
+        out_shape=jax.ShapeDtypeStruct((chunks, GRP, SHARD, ROWS, WIDE), jnp.bfloat16),
+        in_specs=[pl.BlockSpec(memory_space=pl.ANY)],
+        out_specs=pl.BlockSpec(memory_space=pl.ANY),
+        scratch_shapes=gather_sems(chunks),
+        compiler_params=pltpu.CompilerParams(
+            collective_id=0, has_side_effects=True, vmem_limit_bytes=32 << 20
+        ),
+    )(src)
+
+
+class Reduce:
+    def __init__(self, place, src, out, bufs, sems):
+        self.p = place
+        self.src = src
+        self.out = out
+        self.own, self.b1, self.b2, self.b3, self.b4 = bufs
+        (
+            self.ls,
+            self.s1,
+            self.r1,
+            self.s2,
+            self.r2,
+            self.s3,
+            self.r3,
+            self.s4,
+            self.r4,
+        ) = sems
+
+    def local(self, c):
+        p, k = self.p, c % SLOTS
+        return [
+            pltpu.make_async_copy(
+                self.src.at[c, :, p.sets[j]], self.own.at[k, j], self.ls.at[k, j]
+            )
+            for j in range(4)
+        ]
+
+    def other(self, c):
+        p, k = self.p, c % SLOTS
+        return [
+            remote(
+                self.src.at[c, :, flip(p.sets[j], 1)],
+                self.b1.at[k, j],
+                self.s1.at[k, j],
+                self.r1.at[k, j],
+                (p.z, p.sib),
+            )
+            for j in range(4)
+        ]
+
+    def corner(self, c):
+        p, k = self.p, c % SLOTS
+        peers = [(p.z, p.xn), (p.z, p.yn)]
+        return [
+            remote(
+                self.own.at[k, 3, pl.ds(2 * i, 2)],
+                self.b2.at[k, i],
+                self.s2.at[k, i],
+                self.r2.at[k, i],
+                peers[i],
+            )
+            for i in range(2)
+        ]
+
+    def plane(self, c):
+        p, k = self.p, c % SLOTS
+        peers = [(p.z, p.xn), (p.z, p.yn)]
+        return [
+            remote(
+                self.own.at[k, 1 + i],
+                self.b3.at[k, i],
+                self.s3.at[k, i],
+                self.r3.at[k, i],
+                peers[i],
+            )
+            for i in range(2)
+        ]
+
+    def line(self, c):
+        p, k = self.p, c % SLOTS
+        return [
+            remote(
+                self.own.at[k, 0, p.z_peers[i]],
+                self.b4.at[k, i],
+                self.s4.at[k, i],
+                self.r4.at[k, i],
+                (p.z_peers[i], p.s),
+            )
+            for i in range(GRP - 1)
+        ]
+
+    def drain(self, c):
+        sent_all(self.other(c) + self.corner(c) + self.plane(c) + self.line(c))
+
+    def enter(self, c):
+        if c >= SLOTS:
+            self.drain(c - SLOTS)
+        start_all(self.local(c))
+        start_all(self.other(c))
+
+    def add_other(self, c):
+        k = c % SLOTS
+        for copy in self.local(c):
+            copy.wait()
+        recv_all(self.other(c))
+        for j in (3, 2, 1, 0):
+            total = self.own[k, j].astype(jnp.float32) + self.b1[k, j].astype(jnp.float32)
+            self.own[k, j] = total.astype(jnp.bfloat16)
+            if j == 3:
+                start_all(self.corner(c))
+
+    def add_corner(self, c):
+        k = c % SLOTS
+        recv_all(self.corner(c))
+        for j, lo, i in ((2, 0, 0), (1, 2, 1)):
+            total = self.own[k, j, lo : lo + 2].astype(jnp.float32) + self.b2[k, i].astype(
+                jnp.float32
+            )
+            self.own[k, j, lo : lo + 2] = total.astype(jnp.bfloat16)
+        start_all(self.plane(c))
+
+    def add_plane(self, c):
+        k = c % SLOTS
+        recv_all(self.plane(c))
+        total = self.own[k, 0].astype(jnp.float32)
+        total += self.b3[k, 0].astype(jnp.float32)
+        total += self.b3[k, 1].astype(jnp.float32)
+        self.own[k, 0] = total.astype(jnp.bfloat16)
+        start_all(self.line(c))
+
+    def finish(self, c):
+        k = c % SLOTS
+        recv_all(self.line(c))
+        total = self.own[k, 0, self.p.z].astype(jnp.float32)
+        for i in range(GRP - 1):
+            total += self.b4[k, i].astype(jnp.float32)
+        self.out[c] = total
+
+    def step(self, t, chunks):
+        if t + 1 < chunks:
+            self.enter(t + 1)
+        if t < chunks:
+            self.add_other(t)
+        if 0 <= t - 1 < chunks:
+            self.add_corner(t - 1)
+        if 0 <= t - 2 < chunks:
+            self.add_plane(t - 2)
+        if 0 <= t - 3 < chunks:
+            self.finish(t - 3)
+
+
+def reduce_scratch():
+    def buf(*shape):
+        return pltpu.VMEM((SLOTS,) + shape + (ROWS, WIDE), jnp.bfloat16)
+
+    bufs = [buf(4, GRP), buf(4, GRP), buf(2, 2), buf(2, GRP), buf(GRP - 1)]
+    counts = (4, 4, 4, 2, 2, 2, 2, 3, 3)
+    return bufs + [DMA((SLOTS, count)) for count in counts]
+
+
+def reduce_kernel(src, out, *scratch):
+    chunks = src.shape[0]
+    place = Place()
+    barrier, greeted = place.greet()
+    red = Reduce(place, src, out, scratch[:5], scratch[5:])
+    pl.semaphore_wait(barrier, greeted)
+    red.enter(0)
+    for t in range(chunks + 3):
+        red.step(t, chunks)
+    for c in range(max(0, chunks - SLOTS), chunks):
+        red.drain(c)
+
+
+def reduce_call(src):
+    chunks = src.shape[0]
+    return pl.pallas_call(
+        reduce_kernel,
+        out_shape=jax.ShapeDtypeStruct((chunks, ROWS, WIDE), jnp.float32),
+        in_specs=[pl.BlockSpec(memory_space=pl.ANY)],
+        scratch_shapes=reduce_scratch(),
+        compiler_params=pltpu.CompilerParams(
+            collective_id=1, has_side_effects=True, vmem_limit_bytes=48 << 20
+        ),
+    )(src)
+
+
+def pad_cols(mat, width):
+    return jnp.pad(mat, ((0, 0), (0, width - mat.shape[1])))
+
+
+def pad_rows(mat, rows):
+    return jnp.pad(mat, ((0, rows - mat.shape[0]), (0, 0)))
+
+
+def pack(parts, rows):
+    (
+        g_attn,
+        w_query,
+        w_key,
+        w_value,
+        w_outgate,
+        w_lowrank,
+        forget_t,
+        b_forget,
+        g_head,
+        w_output,
+        g_ffn,
+        w_gate,
+        w_up,
+        down_t,
+    ) = parts
+    devs = rows // ROWS
+
+    def spread(mat):
+        cut = mat.reshape(devs, -1, mat.shape[1])
+        return jnp.pad(cut, ((0, 0), (0, ROWS - cut.shape[1]), (0, 0))).reshape(rows, -1)
+
+    misc = jnp.concatenate(
+        [
+            w_lowrank,
+            g_attn[:, None],
+            g_ffn[:, None],
+            spread(g_head[:, None]),
+            jnp.zeros((rows, 13), w_lowrank.dtype),
+            spread(forget_t),
+            spread(b_forget[:, None]),
+        ],
+        axis=1,
+    )
+    mixer = jnp.concatenate(
+        [pad_cols(misc, MISC), w_query, w_key, w_value, w_outgate, w_output], axis=1
+    )
+    heads = -(-mixer.shape[1] // WIDE)
+    mixer = pad_cols(mixer, heads * WIDE).reshape(rows, heads, WIDE)
+    cuts = w_gate.shape[1] // FF_CUT
+    ffn = jnp.concatenate(
+        [mat.reshape(rows, cuts, FF_CUT) for mat in (w_gate, w_up, down_t)], axis=2
+    )
+    return jnp.swapaxes(jnp.concatenate([mixer, ffn], axis=1), 0, 1)
+
+
+def unpack(chunks, sizes):
+    rows = chunks.shape[1]
+    devs = rows // ROWS
+    key_wide, val_wide, rank, forget_rows, head_rows, model = sizes
+    heads = -(-(MISC + 2 * key_wide + 2 * val_wide + model) // WIDE)
+    flat = jnp.swapaxes(chunks[:heads], 0, 1).reshape(rows, heads * WIDE)
+    at = MISC
+    mats = []
+    for wide in (key_wide, key_wide, val_wide, val_wide, model):
+        mats.append(flat[:, at : at + wide])
+        at += wide
+
+    def gathered(lo, hi, keep):
+        return flat[:, lo:hi].reshape(devs, ROWS, hi - lo)[:, :keep].reshape(devs * keep, hi - lo)
+
+    ffn = chunks[heads:]
+    ffn = [
+        jnp.swapaxes(ffn[:, :, i * FF_CUT : (i + 1) * FF_CUT], 0, 1).reshape(rows, -1)
+        for i in range(3)
+    ]
+    return (
+        flat[:, rank],
+        mats[0],
+        mats[1],
+        mats[2],
+        mats[3],
+        flat[:, :rank],
+        gathered(32, 32 + rank, forget_rows),
+        gathered(48, 49, forget_rows)[:, 0],
+        gathered(18, 19, head_rows)[:, 0],
+        mats[4],
+        flat[:, rank + 1],
+        ffn[0],
+        ffn[1],
+        ffn[2],
+    )
+
+
+def plain_shards(
     inputs,
     cotangent,
     lengths,
@@ -297,9 +782,78 @@
     return (out_rows.reshape(inputs.shape), grad_rows.reshape(inputs.shape)) + reduced
 
 
+def kernel_shards(
+    inputs,
+    cotangent,
+    lengths,
+    dealing,
+    g_attn,
+    w_query,
+    w_key,
+    w_value,
+    w_outgate,
+    w_lowrank,
+    w_forget,
+    b_forget,
+    g_head,
+    w_output,
+    g_ffn,
+    w_gate,
+    w_up,
+    w_down,
+):
+    self_index = lax.axis_index("grp") * SHARD + lax.axis_index("shard")
+    seq_dev, max_len, _ = inputs.shape
+    own_given = self_index * seq_dev + jnp.arange(seq_dev, dtype=jnp.int32)
+    own_len = jnp.sum(jnp.where(dealing[None, :] == own_given[:, None], lengths[None, :], 0), axis=1)
+    live = jnp.arange(max_len, dtype=jnp.int32)[None, :] < own_len[:, None]
+    zero_low = jnp.zeros((), jnp.bfloat16)
+    rows_in = jnp.where(live[..., None], inputs, zero_low).reshape(seq_dev * max_len, D)
+    back_in = jnp.where(live[..., None], cotangent, zero_low).reshape(seq_dev * max_len, D)
+    shard_weights = (
+        g_attn,
+        w_query,
+        w_key,
+        w_value,
+        w_outgate,
+        w_lowrank,
+        w_forget.T,
+        b_forget,
+        g_head,
+        w_output,
+        g_ffn,
+        w_gate,
+        w_up,
+        w_down.T,
+    )
+    sizes = (
+        w_query.shape[1],
+        w_value.shape[1],
+        w_lowrank.shape[1],
+        b_forget.shape[0],
+        g_head.shape[0],
+        D,
+    )
+    full = gather_call(pack(shard_weights, ROWS))
+    full = full.reshape(full.shape[0], GRP * SHARD * ROWS, WIDE)
+    weights = list(unpack(full, sizes))
+    weights[6] = weights[6].T
+    weights[13] = weights[13].T
+    out_rows, grad_rows, grads = layer_pass(weights, rows_in, back_in, seq_dev)
+    grads = [grad.astype(jnp.bfloat16) for grad in grads]
+    grads[6] = grads[6].T
+    grads[13] = grads[13].T
+    packed = pack(grads, GRP * SHARD * ROWS)
+    reduced = list(unpack(reduce_call(packed.reshape(packed.shape[0], GRP, SHARD, ROWS, WIDE)), sizes))
+    reduced[6] = reduced[6].T
+    reduced[13] = reduced[13].T
+    return (out_rows.reshape(inputs.shape), grad_rows.reshape(inputs.shape)) + tuple(reduced)
+
+
 def solution(mesh):
+    small = mesh.shape["grp"] == GRP and mesh.shape["shard"] == SHARD
     return jax.shard_map(
-        shards,
+        kernel_shards if small else plain_shards,
         mesh=mesh,
         in_specs=(
             P(("grp", "shard"), None, None),

time: 1960 us -> 674 us (0.34)
  waiting for transfers between devices: 1490 us -> 0 us
  Pallas kernels: 0 us -> 251 us
  blocking collectives: 160 us -> 0 us
  local copies, waits for them, and re-layouts: 66.5 us -> 192 us
    reduce_scatter x8 -> x0, waiting for transfers between devices: 1080 us -> none  [shards(): lax.psum_scatter(grad.astype(jnp.bfloat16), axes, scatter_dimension=dim,...]
    all_gather x8 -> x0, waiting for transfers between devices: 270 us -> none  [shards(): lax.all_gather(weight, axes, axis=dim, tiled=True)]
    pallas_call x0 -> x2, Pallas kernels: none -> 251 us  [the longest x1 127 us: gather_call(): pl.pallas_call(gather_kernel, out_shape=jax.ShapeDtypeStruct((chunks, GRP...]
    unnamed x20 -> x0, waiting for transfers between devices: 136 us -> none
    unnamed x2 -> x0, blocking collectives: 82.2 us -> none
    all_gather x2 -> x0, blocking collectives: 77.7 us -> none  [shards(): lax.all_gather(weight, axes, axis=dim, tiled=True)]
    slice x0 -> x10, local copies, waits for them, and re-layouts: none -> 38.8 us  [the longest x2 21.7 us: unpack(): flat = jnp.swapaxes(chunks[:heads], 0, 1).reshape(rows, heads * WIDE)]
    transpose x0 -> x2, local copies, waits for them, and re-layouts: none -> 34.9 us  [the longest x1 34.9 us: pack(): return jnp.swapaxes(jnp.concatenate([mixer, ffn], axis=1), 0, 1)]
  transfers between devices with their start and end apart: 18 -> 0, of which waited for: 16 -> 0; matrix products, arithmetic and copies ran while one was open for 10% -> 0% of each run, Pallas kernels for 0% -> 0%
where the time goes in v2:
time: 674 us; the launch traced here: 667 us
  Pallas kernels  251 us (37%)
  local copies, waits for them, and re-layouts  192 us (28%)
  matrix products  171 us (25%)
  other arithmetic  49.7 us (7%)
    pallas_call x1, Pallas kernels, gather_call(): pl.pallas_call(gather_kernel, out_shape=jax.ShapeDtypeStruct((chunks, GRP...  127 us
    pallas_call x1, Pallas kernels, reduce_call(): pl.pallas_call(reduce_kernel, out_shape=jax.ShapeDtypeStruct((chunks, ROW...  124 us
    dot_general x10, matrix products, right_transpose(): lax.dot_general(left_mat, right_mat, (((1,), (1,)), ((), ())), preferred_...  58.2 us
    dot_general x10, matrix products, matmul(): return jnp.dot(left_mat, right_mat, preferred_element_type=jnp.float32)  58 us
    unnamed x188, local copies, waits for them, and re-layouts  56.6 us
    dot_general x10, matrix products, rows_contract(): lax.dot_general(left_mat, right_mat, (((0,), (0,)), ((), ())), preferred_...  43.7 us
    transpose x1, local copies, waits for them, and re-layouts, pack(): return jnp.swapaxes(jnp.concatenate([mixer, ffn], axis=1), 0, 1)  34.9 us
    convert_element_type x7, local copies, waits for them, and re-layouts, kernel_shards(): grads = [grad.astype(jnp.bfloat16) for grad in grads]  25.3 us

profile of v2, /device:TPU:0, one launch (start us, length us, event | category | flops | bytes accessed | tf_op | source)
XLA Modules:
  0.0 666.9 jit_solution(5415605012111734056)
XLA Ops:
  11.5 127.2 %shard_map.297 = bf16[17,4,8,32,768]{4,3,2,1,0:T(8,128)(2,1)} custom-call(bf16[17,32,768]{2,1,0:T(8,128)(2,1)S(1)} %maximum_bitcast_fusion.1.src), custom_call_target="tpu_custom_call" | custom-call | tf_op jit(solution)/shard_map/pallas_call | solution.py:443
  138.7 8.6 %slice.146 = bf16[6,4,8,32,768]{4,3,2,1,0:T(8,128)(2,1)} slice(bf16[17,4,8,32,768]{4,3,2,1,0:T(8,128)(2,1)} %shard_map.297), slice={[0:6], [0:4], [0:8], [0:32], [0:768]} | slice | bytes 18874368 | tf_op jit(solution)/shard_map/slice | solution.py:691
  147.3 13.1 %copy.176 = bf16[6,1024,768]{1,2,0:T(8,128)(2,1)} copy(bf16[6,1024,768]{2,1,0:T(8,128)(2,1)} %bitcast.340) | data formatting | bytes 18874368 | tf_op jit(solution)/shard_map/slice | solution.py:691
  209.3 9.0 %multiply_convert_fusion.3 = (bf16[768,1024]{1,0:T(8,128)(2,1)S(1)}, f32[768,1024]{1,0:T(8,128)}, f32[768,1024]{1,0:T(8,128)}) fusion(f32[1024]{0:T(1024)S(1)} %bitcast.427, f32[768,1024]{1,0:T(8,128)} %bitcast.390, f32[768,1024]{1,0:T(8,128)} %bitcast.389, bf16[768,1024]{1,0:T(8,128)(2,1)} %copy-done.18, bf16[1024,4608]{0,1:T(8,128)(2,1)} %bitcast.359), kind=kOutput, calls=%fused_computation.52 | convolution fusion | flops 1616904192 | bytes 17829888 | tf_op jit(solution)/shard_map/dot_general | solution.py:28
  230.2 6.3 fusion.102
  236.5 8.6 %copy.223 = bf16[11,1024,256]{1,2,0:T(8,128)(2,1)} copy(bf16[11,1024,256]{2,1,0:T(8,128)(2,1)} %get-tuple-element.107) | data formatting | bytes 11534336
  245.1 11.2 %fusion.108 = f32[768,2816]{1,0:T(8,128)} fusion(bf16[768,1024]{1,0:T(8,128)(2,1)} %multiply_convert_fusion.2, bf16[1024,2816]{0,1:T(8,128)(2,1)} %bitcast.380), kind=kOutput, calls=%fused_computation.228 | convolution fusion | flops 4429185024 | bytes 15990784 | tf_op jit(solution)/shard_map/dot_general | solution.py:28
  256.3 8.3 %copy.222 = bf16[11,1024,256]{1,2,0:T(8,128)(2,1)} copy(bf16[11,1024,256]{2,1,0:T(8,128)(2,1)} %get-tuple-element.108) | data formatting | bytes 11534336
  264.5 11.2 %fusion.107 = f32[768,2816]{1,0:T(8,128)} fusion(bf16[768,1024]{1,0:T(8,128)(2,1)} %multiply_convert_fusion.2, bf16[1024,2816]{0,1:T(8,128)(2,1)} %bitcast.382), kind=kOutput, calls=%fused_computation.227 | convolution fusion | flops 4429185024 | bytes 15990784 | tf_op jit(solution)/shard_map/dot_general | solution.py:28
  275.7 8.3 %copy.224 = bf16[11,1024,256]{1,2,0:T(8,128)(2,1)} copy(bf16[11,1024,256]{2,1,0:T(8,128)(2,1)} %get-tuple-element.106) | data formatting | bytes 11534336
  285.6 17.9 %multiply_convert_fusion = (bf16[768,2816]{1,0:T(8,128)(2,1)}, bf16[768,2816]{1,0:T(8,128)(2,1)}, bf16[768,2816]{1,0:T(8,128)(2,1)}) fusion(f32[768,2816]{1,0:T(8,128)} %fusion.107, f32[768,2816]{1,0:T(8,128)} %fusion.108, bf16[768,1024]{1,0:T(8,128)(2,1)S(1)} %bitcast.376, bf16[1024,2816]{0,1:T(8,128)(2,1)} %bitcast.378), kind=kOutput, calls=%fused_computation.5 | convolution fusion | flops 4463788032 | bytes 37617664 | tf_op jit(solution)/shard_map/dot_general | solution.py:38
  303.6 8.1 %fusion.109 = f32[768,1024]{1,0:T(8,128)S(1)} fusion(bf16[768,2816]{1,0:T(8,128)(2,1)} %get-tuple-element.104, bf16[1024,2816]{0,1:T(8,128)(2,1)} %bitcast.383), kind=kOutput, calls=%fused_computation.229 | convolution fusion | flops 4429185024 | bytes 13238272 | tf_op jit(solution)/shard_map/dot_general | solution.py:38
  311.7 7.8 %multiply_reduce_fusion.1 = (bf16[1024]{0:T(1024)(128)(2,1)S(1)}, f32[768]{0:T(1024)S(1)}, f32[768,1024]{1,0:T(8,128)S(1)}) fusion(f32[768,1024]{1,0:T(8,128)S(1)} %copy-done.25, f32[768]{0:T(1024)S(1)} %fusion.93, f32[1024]{0:T(1024)S(1)} %bitcast.421, f32[768,1024]{1,0:T(8,128)S(1)} %fusion.109, bf16[768,2816]{1,0:T(8,128)(2,1)S(1)} %copy-done.81, ...), kind=kOutput, calls=%fused_computation.44 | convolution fusion | flops 4434688000 | bytes 19542016 | tf_op jit(solution)/shard_map/dot_general | solution.py:38
  405.3 8.2 %pad.53 = bf16[1024,4608]{0,1:T(8,128)(2,1)} pad(bf16[1024,4224]{0,1:T(8,128)(2,1)} %convert_dynamic-update-slice_fusion, bf16[]{:T(256)} %constant.53.clone.1), padding=0_0x0_384 | pad | bytes 18087938 | tf_op jit(solution)/shard_map/jit(_pad)/pad | solution.py:632
  413.5 9.2 %convolution_convert_fusion.2 = bf16[1024,2816]{1,0:T(8,128)(2,1)} fusion(bf16[768,1024]{1,0:T(8,128)(2,1)S(1)} %copy-done.48, bf16[768,2816]{1,0:T(8,128)(2,1)} %get-tuple-element.104), kind=kOutput, calls=%fused_computation.11 | convolution fusion | flops 4432068608 | bytes 11665408 | tf_op jit(solution)/shard_map/dot_general | solution.py:32
  422.7 8.3 %copy.206 = bf16[1024,2816]{0,1:T(8,128)(2,1)} copy(bf16[1024,2816]{1,0:T(8,128)(2,1)} %convolution_convert_fusion.2) | data formatting | bytes 11534336 | tf_op jit(solution)/shard_map/convert_element_type | solution.py:843
  431.0 8.8 %convolution_convert_fusion.1 = bf16[1024,2816]{1,0:T(8,128)(2,1)} fusion(bf16[768,1024]{1,0:T(8,128)(2,1)S(1)} %copy-done.48, bf16[768,2816]{1,0:T(8,128)(2,1)} %get-tuple-element.103), kind=kOutput, calls=%fused_computation.10 | convolution fusion | flops 4432068608 | bytes 11665408 | tf_op jit(solution)/shard_map/dot_general | solution.py:32
  439.8 8.4 %copy.207 = bf16[1024,2816]{0,1:T(8,128)(2,1)} copy(bf16[1024,2816]{1,0:T(8,128)(2,1)} %convolution_convert_fusion.1) | data formatting | bytes 11534336 | tf_op jit(solution)/shard_map/convert_element_type | solution.py:843
  448.2 8.7 %convolution_convert_fusion = bf16[1024,2816]{1,0:T(8,128)(2,1)} fusion(bf16[768,1024]{1,0:T(8,128)(2,1)S(1)} %bitcast.377, bf16[768,2816]{1,0:T(8,128)(2,1)} %get-tuple-element.105), kind=kOutput, calls=%fused_computation.9 | convolution fusion | flops 4432068608 | bytes 11665408 | tf_op jit(solution)/shard_map/dot_general | solution.py:32
  457.0 8.3 %copy.208 = bf16[1024,2816]{0,1:T(8,128)(2,1)} copy(bf16[1024,2816]{1,0:T(8,128)(2,1)} %convolution_convert_fusion) | data formatting | bytes 11534336 | tf_op jit(solution)/shard_map/convert_element_type | solution.py:843
  465.3 20.7 %maximum_bitcast_fusion = bf16[17,1024,768]{1,2,0:T(8,128)(2,1)} fusion(bf16[1024,11,256]{0,2,1:T(8,128)(2,1)} %bitcast.353, bf16[1024,11,256]{0,2,1:T(8,128)(2,1)} %bitcast.352, bf16[1024,11,256]{0,2,1:T(8,128)(2,1)} %bitcast.351, bf16[1024,6,768]{0,2,1:T(8,128)(2,1)} %bitcast.339), kind=kLoop, calls=%fused_computation | loop fusion | flops 106954752 | bytes 53477376 | tf_op jit(solution)/shard_map/transpose | solution.py:683
  486.0 34.9 %copy.209 = bf16[17,1024,768]{2,1,0:T(8,128)(2,1)} copy(bf16[17,1024,768]{1,2,0:T(8,128)(2,1)} %maximum_bitcast_fusion) | data formatting | bytes 53477376 | tf_op jit(solution)/shard_map/transpose | solution.py:683
  520.9 124.0 %shard_map.298 = f32[17,32,768]{2,1,0:T(8,128)S(1)} custom-call(bf16[17,4,8,32,768]{4,3,2,1,0:T(8,128)(2,1)} %bitcast.338), custom_call_target="tpu_custom_call" | custom-call | tf_op jit(solution)/shard_map/pallas_call | solution.py:620
  657.0 9.8 %add_convert_fusion.1 = bf16[768,1024]{1,0:T(8,128)(2,1)} fusion(f32[768,1024]{1,0:T(8,128)S(1)} %copy-done.26, bf16[768,2816]{1,0:T(8,128)(2,1)} %get-tuple-element.105, bf16[1024,2816]{0,1:T(8,128)(2,1)} %bitcast.379), kind=kOutput, calls=%fused_computation.49 | convolution fusion | flops 4430757888 | bytes 14811136 | tf_op jit(solution)/shard_map/dot_general | solution.py:28
  (320 shorter events, 170.0 us)
Async XLA Ops:
  147.3 15.2 %copy-start.73 = (s32[128]{0:T(128)S(1)}, s32[128]{0:T(128)}, u32[]{:S(2)}) copy-start(s32[128]{0:T(128)} %param.20) | copy-start | bytes 1540
  147.3 15.2 %copy-start.74 = (s32[128]{0:T(128)S(1)}, s32[128]{0:T(128)}, u32[]{:S(2)}) copy-start(s32[128]{0:T(128)} %param.21) | copy-start | bytes 1540
  147.3 15.4 %copy-start.45 = (bf16[4,192,1024]{2,1,0:T(8,128)(2,1)S(1)}, bf16[4,192,1024]{2,1,0:T(8,128)(2,1)}, u32[]{:S(2)}) copy-start(bf16[4,192,1024]{2,1,0:T(8,128)(2,1)} %param.18) | copy-start | bytes 4718596
  162.5 11.2 %copy-start.57 = (f32[1024,1]{0,1:T(1,128)}, f32[1024,1]{0,1:T(1,128)S(1)}, u32[]{:S(2)}) copy-start(f32[1024,1]{0,1:T(1,128)S(1)} %get-tuple-element.113) | copy-start | bytes 12292
  163.4 10.2 %copy-start = (bf16[4,192,1024]{2,1,0:T(8,128)(2,1)}, bf16[4,192,1024]{2,1,0:T(8,128)(2,1)S(1)}, u32[]{:S(2)}) copy-start(bf16[4,192,1024]{2,1,0:T(8,128)(2,1)S(1)} %get-tuple-element.102) | copy-start | bytes 4718596
  174.1 4.9 copy-start.36
  181.5 8.1 %copy-start.29 = (bf16[12,64,4,128]{3,1,2,0:T(8,128)(2,1)}, bf16[12,64,4,128]{3,1,2,0:T(8,128)(2,1)S(1)}, u32[]{:S(2)}) copy-start(bf16[12,64,4,128]{3,1,2,0:T(8,128)(2,1)S(1)} %get-tuple-element.126) | copy-start | bytes 2359300
  181.5 13.7 %copy-start.15 = (bf16[12,64,4,128]{3,1,2,0:T(8,128)(2,1)}, bf16[12,64,4,128]{3,1,2,0:T(8,128)(2,1)S(1)}, u32[]{:S(2)}) copy-start(bf16[12,64,4,128]{3,1,2,0:T(8,128)(2,1)S(1)} %get-tuple-element.127) | copy-start | bytes 2359300
  189.6 6.9 %copy-start.11 = (bf16[12,64,4,256]{3,2,1,0:T(4,128)(2,1)}, bf16[12,64,4,256]{3,2,1,0:T(4,128)(2,1)S(1)}, u32[]{:S(2)}) copy-start(bf16[12,64,4,256]{3,2,1,0:T(4,128)(2,1)S(1)} %reshape.484) | copy-start | bytes 4718596
  209.3 9.0 %copy-start.1 = (bf16[4,192,1024]{2,1,0:T(8,128)(2,1)S(1)}, bf16[4,192,1024]{2,1,0:T(8,128)(2,1)}, u32[]{:S(2)}) copy-start(bf16[4,192,1024]{2,1,0:T(8,128)(2,1)} %copy-done) | copy-start | bytes 4718596
  218.3 4.2 copy-start.67
  224.3 5.9 slice-start
  275.7 8.3 %copy-start.72 = (pred[4,192]{1,0:T(4,128)(4,1)S(1)}, pred[4,192]{1,0:T(4,128)(4,1)}, u32[]{:S(2)}) copy-start(pred[4,192]{1,0:T(4,128)(4,1)} %copy-done.71) | copy-start | bytes 2308
  285.6 33.9 %copy-start.38 = (bf16[4,192,1024]{2,1,0:T(8,128)(2,1)}, bf16[4,192,1024]{2,1,0:T(8,128)(2,1)S(1)}, u32[]{:S(2)}) copy-start(bf16[4,192,1024]{2,1,0:T(8,128)(2,1)S(1)} %broadcast_select_fusion) | copy-start | bytes 4718596
  303.6 8.1 %copy-start.25 = (f32[768,1024]{1,0:T(8,128)S(1)}, f32[768,1024]{1,0:T(8,128)}, u32[]{:S(2)}) copy-start(f32[768,1024]{1,0:T(8,128)} %copy-done.24) | copy-start | bytes 9437188
  303.6 8.1 %copy-start.81 = (bf16[768,2816]{1,0:T(8,128)(2,1)S(1)}, bf16[768,2816]{1,0:T(8,128)(2,1)}, u32[]{:S(2)}) copy-start(bf16[768,2816]{1,0:T(8,128)(2,1)} %get-tuple-element.103) | copy-start | bytes 12976132
  320.3 9.3 %copy-start.22 = (f32[768,1024]{1,0:T(8,128)}, f32[768,1024]{1,0:T(8,128)S(1)}, u32[]{:S(2)}) copy-start(f32[768,1024]{1,0:T(8,128)S(1)} %fusion.4) | copy-start | bytes 9437188
  338.8 10.4 %copy-start.13 = (bf16[12,64,4,256]{3,1,2,0:T(8,128)(2,1)}, bf16[12,64,4,256]{3,1,2,0:T(8,128)(2,1)S(1)}, u32[]{:S(2)}) copy-start(bf16[12,64,4,256]{3,1,2,0:T(8,128)(2,1)S(1)} %fusion.5) | copy-start | bytes 4718596
  355.8 4.2 copy-start.49
  384.7 5.6 copy-start.37
  405.3 8.2 %copy-start.48 = (bf16[768,1024]{1,0:T(8,128)(2,1)S(1)}, bf16[768,1024]{1,0:T(8,128)(2,1)}, u32[]{:S(2)}) copy-start(bf16[768,1024]{1,0:T(8,128)(2,1)} %multiply_convert_fusion.2) | copy-start | bytes 4718596
  439.8 8.4 %copy-start.39 = (bf16[4,192,1024]{2,1,0:T(8,128)(2,1)S(1)}, bf16[4,192,1024]{2,1,0:T(8,128)(2,1)}, u32[]{:S(2)}) copy-start(bf16[4,192,1024]{2,1,0:T(8,128)(2,1)} %copy-done.38) | copy-start | bytes 4718596
  645.0 7.0 %copy-start.69 = (f32[768]{0:T(1024)S(1)}, f32[768]{0:T(1024)}, u32[]{:S(2)}) copy-start(f32[768]{0:T(1024)} %copy-done.68) | copy-start | bytes 9220
  652.0 5.0 copy-start.26
  (61 other events, 151.9 us)
